TPU v7x, 512 devices: a whole 4x4x16 slice. The times are simulated.
512 devices in a mesh: wave: 16 (over z), tile: 32 (over y, x, core).
Axes of the slice: x: 4, y: 4, z: 16, core: 2. Of those that a mesh axis runs over, the one named last changes fastest.
Arguments:
- warm_start: float32 [16, 2, 1024, 1024], P('wave', None, 'tile'), may hold values from -30 to 30
- class_map: int32 [1024, 1024], P('tile'), may hold values from 0 to 7
- conductivities: float32 [8], replicated, may hold values from 0.1 to 10
- wavenumbers: float32 [16], P('wave'), may hold values from 0.05 to 2
- weights: float32 [16], P('wave'), may hold values from 0.1 to 1
- source_row: int32 [2], replicated, may hold values from 0 to 1023
- source_col: int32 [2], replicated, may hold values from 0 to 1023
- electrode_row: int32 [64], replicated, may hold values from 0 to 1023
Outputs:
- potentials: float32 [2, 1024, 1024], P(None, 'tile', 'wave')
- readings: float32 [2, 64], replicated
All inputs are finite; a program needn't handle non-finite values.
Results may differ from a plain program's by a relative error of at most 0.0003.
Values sent between devices are 32-bit elements; how exact they have to be, the bound alone decides.
A program may use at most 64 MiB of HBM per device.

v0:
```python
import jax
import jax.numpy as jnp
from jax import lax
from jax.sharding import PartitionSpec as P

ITERS = 3


source_strength = 50.0


def extended(shard, sides, width):
    for axis, dim in sides:
        size, length = (lax.axis_size(axis), shard.shape[dim])
        up = [(i, (i + 1) % size) for i in range(size - 1)]
        down = [(j, i) for i, j in up]
        last = lax.slice_in_dim(shard, length - width, length, axis=dim)
        initial = lax.slice_in_dim(shard, 0, width, axis=dim)
        before = lax.ppermute(last, axis, up)
        after = lax.ppermute(initial, axis, down)
        shard = jnp.concatenate([before, shard, after], axis=dim)
    return shard


def harmonic(left_val, right_val):
    return 2.0 * left_val * right_val / (left_val + right_val)


def shards(
    warm_start,
    class_map,
    conductivities,
    wavenumbers,
    weights,
    source_row,
    source_col,
    electrode_row,
):
    rows_here = class_map.shape[0]
    depth = class_map.shape[1]
    n_class = conductivities.shape[0]
    class_ids = jnp.arange(n_class, dtype=jnp.int32)
    sigma = jnp.sum(
        jnp.where(class_map[None] == class_ids[:, None, None], conductivities[:, None, None], 0.0),
        axis=0,
    )
    sigma_rim = extended(sigma, (("tile", 0),), 1)
    face_row = harmonic(sigma_rim[:-1], sigma_rim[1:])
    face_up = face_row[:-1]
    face_down = face_row[1:]
    col_inner = harmonic(sigma[:, :-1], sigma[:, 1:])
    face_left = jnp.concatenate([jnp.zeros((rows_here, 1), jnp.float32), col_inner], axis=1)
    face_right = jnp.concatenate([col_inner, sigma[:, -1:]], axis=1)
    base = face_up + face_down + face_left + face_right
    wave_num = wavenumbers[0]
    diag = base + wave_num * wave_num * sigma
    global_row = lax.axis_index("tile") * rows_here + jnp.arange(rows_here, dtype=jnp.int32)
    col_ids = jnp.arange(depth, dtype=jnp.int32)
    hits = (global_row[None, :, None] == source_row[:, None, None]) & (
        col_ids[None, None, :] == source_col[:, None, None]
    )
    rhs = source_strength * hits.astype(jnp.float32)

    def operate(values):
        row_padded = extended(values, (("tile", 1),), 1)
        col_padded = jnp.pad(values, ((0, 0), (0, 0), (1, 1)))
        return (
            diag * values
            - face_up * row_padded[:, :-2]
            - face_down * row_padded[:, 2:]
            - face_left * col_padded[:, :, :-2]
            - face_right * col_padded[:, :, 2:]
        )

    def local_inner(first, second):
        return jnp.sum(first * second, axis=(1, 2))

    def resid_inner(residual, scaled):
        return lax.psum(local_inner(residual, scaled), "tile")[:, None, None]

    field = warm_start[0]
    residual = rhs - operate(field)
    scaled = residual / diag
    direction = scaled
    gamma_now = resid_inner(residual, scaled)
    for iteration in range(ITERS):
        image = operate(direction)
        curve = lax.psum(local_inner(direction, image), "tile")[:, None, None]
        step_size = gamma_now / curve
        field = field + step_size * direction
        residual = residual - step_size * image
        scaled = residual / diag
        gamma_next = resid_inner(residual, scaled)
        direction = scaled + gamma_next / gamma_now * direction
        gamma_now = gamma_next
    weighted = weights[0] * field
    picker = (global_row[:, None] == electrode_row[None, :]).astype(jnp.float32)
    local_read = jnp.dot(
        weighted[:, :, 0],
        picker,
        precision=lax.Precision.HIGHEST,
        preferred_element_type=jnp.float32,
    )
    readings = lax.psum(local_read, ("wave", "tile"))
    summed = lax.psum(weighted, "wave")
    share = depth // lax.axis_size("wave")
    potentials = lax.dynamic_slice_in_dim(summed, lax.axis_index("wave") * share, share, 2)
    return (potentials, readings)


def solution(mesh):
    return jax.shard_map(
        shards,
        mesh=mesh,
        in_specs=(
            P("wave", None, "tile", None),
            P("tile", None),
            P(),
            P("wave"),
            P("wave"),
            P(),
            P(),
            P(),
        ),
        out_specs=(P(None, "tile", "wave"), P()),
        check_vma=False,
    )
```

profile of v0, /device:TPU:2, one launch (start us, length us, event | category | flops | bytes accessed | tf_op | source)
XLA Modules:
  0.0 508.0 jit_solution(10058735618531560873)
XLA Ops:
  7.2 1.1 select_reduce_fusion
  8.3 1.9 collective-permute-start
  10.3 3.6 collective-permute-start.1
  13.9 1.9 collective-permute-start.2
  15.9 5.6 %collective-permute-start.3 = (f32[2,1,1024]{2,1,0:T(1,128)S(1)}, f32[2,1,1024]{2,1,0:T(1,128)S(1)}, u32[]{:S(2)}, u32[]{:S(2)}) collective-permute-start(f32[2,1,1024]{2,1,0:T(1,128)S(1)} %get-tuple-element.22), channel_id=1, source_target_pairs={{1,0},{2,1},{3,2},{4,3},{5,4},{6,5},{7,6},{8,7},{9,8},{10,9},{11,1... | collective-permute-start | bytes 24584 | tf_op jit(solution)/shard_map/ppermute | solution.py:20
  21.6 0.6 copy-done.2
  22.3 0.6 copy-done.3
  23.9 0.2 broadcast_divide_fusion
  24.2 1.9 collective-permute-start.4
  26.1 3.6 collective-permute-start.5
  29.8 1.3 collective-permute-done.5
  31.1 0.3 multiply_reduce_fusion.3
  31.4 59.2 %all-reduce.5 = (f32[2]{0:T(128)S(1)}, f32[2]{0:T(128)S(1)}) all-reduce(f32[2]{0:T(128)S(1)} %get-tuple-element.3, f32[2]{0:T(128)S(1)} %get-tuple-element.2), channel_id=1, replica_groups=mesh['wave'=16,'tile'=32] {'tile'}, use_global_device_ids=true, to_apply=%region_2.3 | all-reduce | flops 4 | bytes 32 | tf_op jit(solution)/shard_map/psum | solution.py:79
  90.6 0.2 multiply_reduce_fusion.2
  90.8 62.7 %psum.58 = f32[2]{0:T(128)S(1)} all-reduce(f32[2]{0:T(128)S(1)} %get-tuple-element.8), channel_id=1, replica_groups=mesh['wave'=16,'tile'=32] {'tile'}, use_global_device_ids=true, to_apply=%region_6.7 | all-reduce | flops 2 | bytes 16 | tf_op jit(solution)/shard_map/psum | solution.py:79
  153.6 1.9 collective-permute-start.6
  155.5 7.0 %collective-permute-start.7 = (f32[2,1,1024]{2,1,0:T(1,128)S(1)}, f32[2,1,1024]{2,1,0:T(1,128)S(1)}, u32[]{:S(2)}, u32[]{:S(2)}) collective-permute-start(f32[2,1,1024]{2,1,0:T(1,128)S(1)} %get-tuple-element.18), channel_id=1, source_target_pairs={{1,0},{2,1},{3,2},{4,3},{5,4},{6,5},{7,6},{8,7},{9,8},{10,9},{11,1... | collective-permute-start | bytes 24584 | tf_op jit(solution)/shard_map/ppermute | solution.py:20
  162.5 1.3 collective-permute-done.7
  163.8 0.3 multiply_reduce_fusion.1
  164.1 59.2 %psum.59 = f32[2]{0:T(128)S(1)} all-reduce(f32[2]{0:T(128)S(1)} %get-tuple-element.6), channel_id=1, replica_groups=mesh['wave'=16,'tile'=32] {'tile'}, use_global_device_ids=true, to_apply=%region_8.9 | all-reduce | flops 2 | bytes 16 | tf_op jit(solution)/shard_map/psum | solution.py:88
  223.3 0.2 multiply_reduce_fusion
  223.5 62.7 %psum.60 = f32[2]{0:T(128)S(1)} all-reduce(f32[2]{0:T(128)S(1)} %multiply_reduce_fusion), channel_id=1, replica_groups=mesh['wave'=16,'tile'=32] {'tile'}, use_global_device_ids=true, to_apply=%region_10.11 | all-reduce | flops 2 | bytes 16 | tf_op jit(solution)/shard_map/psum | solution.py:79
  286.4 1.9 collective-permute-start.8
  288.3 7.0 %collective-permute-start.9 = (f32[2,1,1024]{2,1,0:T(1,128)S(1)}, f32[2,1,1024]{2,1,0:T(1,128)S(1)}, u32[]{:S(2)}, u32[]{:S(2)}) collective-permute-start(f32[2,1,1024]{2,1,0:T(1,128)S(1)} %get-tuple-element.16), channel_id=1, source_target_pairs={{1,0},{2,1},{3,2},{4,3},{5,4},{6,5},{7,6},{8,7},{9,8},{10,9},{11,1... | collective-permute-start | bytes 24584 | tf_op jit(solution)/shard_map/ppermute | solution.py:20
  295.3 1.3 collective-permute-done.9
  296.6 0.3 fusion.17
  297.6 59.2 %psum.61 = f32[2]{0:T(128)S(1)} all-reduce(f32[2]{0:T(128)S(1)} %fusion.17), channel_id=1, replica_groups=mesh['wave'=16,'tile'=32] {'tile'}, use_global_device_ids=true, to_apply=%region_12.13 | all-reduce | flops 2 | bytes 16 | tf_op jit(solution)/shard_map/psum | solution.py:88
  357.1 0.6 copy-done
  357.8 0.6 copy-done.4
  358.6 110.4 %psum.63 = f32[2,64]{1,0:T(2,128)} all-reduce(f32[2,64]{1,0:T(2,128)S(1)} %fusion.35), channel_id=1, replica_groups=mesh['wave'=16,'tile'=32] {'wave','tile'}, use_global_device_ids=true, to_apply=%region_14.15 | all-reduce | flops 128 | bytes 1024 | tf_op jit(solution)/shard_map/psum | solution.py:104
  469.1 30.6 %all-reduce.8.cloned.1.call-done = f32[2,32,1024]{2,1,0:T(8,128)} async-done(((f32[2,32,1024]{2,1,0:T(8,128)}), f32[2,32,1024]{2,1,0:T(8,128)}) %all-reduce.8.cloned.1.call-update) | async-done | bytes 262160 | tf_op jit(solution)/shard_map/psum | solution.py:105
  499.7 1.4 constant_dynamic-slice_fusion
  (37 shorter events, 1.4 us)
Async XLA Ops:
  7.2 6.8 %copy-start.1 = (f32[1,2,32,1024]{3,2,1,0:T(8,128)S(1)}, f32[1,2,32,1024]{3,2,1,0:T(8,128)}, u32[]{:S(2)}) copy-start(f32[1,2,32,1024]{3,2,1,0:T(8,128)} %param.8) | copy-start | bytes 786436
  8.3 15.4 %collective-permute-start = (f32[1,1024]{1,0:T(1,128)S(1)}, f32[1,1024]{1,0:T(1,128)S(1)}, u32[]{:S(2)}, u32[]{:S(2)}) collective-permute-start(f32[1,1024]{1,0:T(1,128)S(1)} %get-tuple-element.26), channel_id=1, source_target_pairs={{0,1},{1,2},{2,3},{3,4},{4,5},{5,6},{6,7},{7,8},{8,9},{9,10},{10,1... | collective-permute-start | bytes 12296 | tf_op jit(solution)/shard_map/ppermute | solution.py:19
  10.3 13.4 %collective-permute-start.1 = (f32[1,1024]{1,0:T(1,128)S(1)}, f32[1,1024]{1,0:T(1,128)S(1)}, u32[]{:S(2)}, u32[]{:S(2)}) collective-permute-start(f32[1,1024]{1,0:T(1,128)S(1)} %get-tuple-element.27), channel_id=1, source_target_pairs={{1,0},{2,1},{3,2},{4,3},{5,4},{6,5},{7,6},{8,7},{9,8},{10,9},{11,1... | collective-permute-start | bytes 12296 | tf_op jit(solution)/shard_map/ppermute | solution.py:20
  13.9 9.9 %collective-permute-start.2 = (f32[2,1,1024]{2,1,0:T(1,128)S(1)}, f32[2,1,1024]{2,1,0:T(1,128)S(1)}, u32[]{:S(2)}, u32[]{:S(2)}) collective-permute-start(f32[2,1,1024]{2,1,0:T(1,128)S(1)} %get-tuple-element.21), channel_id=1, source_target_pairs={{0,1},{1,2},{2,3},{3,4},{4,5},{5,6},{6,7},{7,8},{8,9},{9,10},{10,1... | collective-permute-start | bytes 24584 | tf_op jit(solution)/shard_map/ppermute | solution.py:19
  15.9 8.0 %collective-permute-start.3 = (f32[2,1,1024]{2,1,0:T(1,128)S(1)}, f32[2,1,1024]{2,1,0:T(1,128)S(1)}, u32[]{:S(2)}, u32[]{:S(2)}) collective-permute-start(f32[2,1,1024]{2,1,0:T(1,128)S(1)} %get-tuple-element.22), channel_id=1, source_target_pairs={{1,0},{2,1},{3,2},{4,3},{5,4},{6,5},{7,6},{8,7},{9,8},{10,9},{11,1... | collective-permute-start | bytes 24584 | tf_op jit(solution)/shard_map/ppermute | solution.py:20
  21.6 0.7 copy-start.2
  22.2 0.7 copy-start.3
  24.2 5.6 %collective-permute-start.4 = (f32[2,1,1024]{2,1,0:T(1,128)S(1)}, f32[2,1,1024]{2,1,0:T(1,128)S(1)}, u32[]{:S(2)}, u32[]{:S(2)}) collective-permute-start(f32[2,1,1024]{2,1,0:T(1,128)S(1)} %get-tuple-element.19), channel_id=1, source_target_pairs={{0,1},{1,2},{2,3},{3,4},{4,5},{5,6},{6,7},{7,8},{8,9},{9,10},{10,1... | collective-permute-start | bytes 24584 | tf_op jit(solution)/shard_map/ppermute | solution.py:19
  26.1 5.0 collective-permute-start.5
  153.6 8.9 %collective-permute-start.6 = (f32[2,1,1024]{2,1,0:T(1,128)S(1)}, f32[2,1,1024]{2,1,0:T(1,128)S(1)}, u32[]{:S(2)}, u32[]{:S(2)}) collective-permute-start(f32[2,1,1024]{2,1,0:T(1,128)S(1)} %get-tuple-element.17), channel_id=1, source_target_pairs={{0,1},{1,2},{2,3},{3,4},{4,5},{5,6},{6,7},{7,8},{8,9},{9,10},{10,1... | collective-permute-start | bytes 24584 | tf_op jit(solution)/shard_map/ppermute | solution.py:19
  155.5 8.3 %collective-permute-start.7 = (f32[2,1,1024]{2,1,0:T(1,128)S(1)}, f32[2,1,1024]{2,1,0:T(1,128)S(1)}, u32[]{:S(2)}, u32[]{:S(2)}) collective-permute-start(f32[2,1,1024]{2,1,0:T(1,128)S(1)} %get-tuple-element.18), channel_id=1, source_target_pairs={{1,0},{2,1},{3,2},{4,3},{5,4},{6,5},{7,6},{8,7},{9,8},{10,9},{11,1... | collective-permute-start | bytes 24584 | tf_op jit(solution)/shard_map/ppermute | solution.py:20
  286.4 8.9 %collective-permute-start.8 = (f32[2,1,1024]{2,1,0:T(1,128)S(1)}, f32[2,1,1024]{2,1,0:T(1,128)S(1)}, u32[]{:S(2)}, u32[]{:S(2)}) collective-permute-start(f32[2,1,1024]{2,1,0:T(1,128)S(1)} %get-tuple-element.15), channel_id=1, source_target_pairs={{0,1},{1,2},{2,3},{3,4},{4,5},{5,6},{6,7},{7,8},{8,9},{9,10},{10,1... | collective-permute-start | bytes 24584 | tf_op jit(solution)/shard_map/ppermute | solution.py:19
  288.3 8.3 %collective-permute-start.9 = (f32[2,1,1024]{2,1,0:T(1,128)S(1)}, f32[2,1,1024]{2,1,0:T(1,128)S(1)}, u32[]{:S(2)}, u32[]{:S(2)}) collective-permute-start(f32[2,1,1024]{2,1,0:T(1,128)S(1)} %get-tuple-element.16), channel_id=1, source_target_pairs={{1,0},{2,1},{3,2},{4,3},{5,4},{6,5},{7,6},{8,7},{9,8},{10,9},{11,1... | collective-permute-start | bytes 24584 | tf_op jit(solution)/shard_map/ppermute | solution.py:20
  357.0 0.7 copy-start
  357.1 142.7 %all-reduce.8.cloned.1.call-start = ((), (), s32[]{:S(2)}) async-start(), calls=%async_computation | async-start | bytes 524288 | tf_op jit(solution)/shard_map/psum | solution.py:105
  357.8 0.7 copy-start.4
Sparse Core Ops, SparseCore 0:
  360.2 139.4 all-reduce.7
where the time goes:
time: 509 us; the launch traced here: 508 us
  blocking collectives  413 us (81%)
  starting transfers between devices  36.4 us (7%)
  waiting for transfers between devices  34.8 us (7%)
  between operations  15.6 us (3%)
    psum x3, blocking collectives, resid_inner(): return lax.psum(local_inner(residual, scaled), 'tile')[:, None, None]  184 us
    psum x2, blocking collectives, shards(): curve = lax.psum(local_inner(direction, image), 'tile')[:, None, None]  118 us
    psum x1, blocking collectives, shards(): readings = lax.psum(local_read, ('wave', 'tile'))  110 us
    psum x1, waiting for transfers between devices, shards(): summed = lax.psum(weighted, 'wave')  30.6 us
    ppermute x5, starting transfers between devices, extended(): after = lax.ppermute(initial, axis, down)  26.8 us
  transfers between devices with their start and end apart: 11, of which 4 were waited for; matrix products, arithmetic and copies ran while one was open for 0% of the time, Pallas kernels for 0%

commit v1 on v0

v1 whole, which is shorter than its diff:
```python
import functools

import jax
import jax.numpy as jnp
from jax import lax
from jax.experimental import pallas as pl
from jax.experimental.pallas import tpu as pltpu
from jax.sharding import PartitionSpec as P

SOURCE_STRENGTH = 50.0
MESH = pl.DeviceIdType.MESH

WAVES = 16
TILES = 32
ROWS = 32
COLS = 1024
EXT = 40
LANES = 128

FIRST = {6: (5, 7, 8), -6: (-7, -5), 3: (2, 4), -3: (-4, -2), 0: (-1, 1)}
FIRST_LIST = [(c, o) for c, offsets in FIRST.items() for o in offsets]
SECOND_LIST = [c for c in FIRST if c != 0]


def harmonic(a, b):
    return 2.0 * a * b / (a + b)


def kernel(
    warm, cls, cond, wn, wt, srow, scol, erow,
    pot, read,
    xbuf, cbuf, ebuf, cond_s, wn_s, wt_s, srow_s, scol_s,
    halo_out, halo_in, pack_x, pack_y, slots_x, slots_y,
    chunks, got_first, sums, got_second, mine, slots_r,
    in_sem, halo_send, halo_recv, x_send, x_recv, y_send, y_recv,
    first_send, first_recv, second_send, second_recv, r_send, r_recv,
):
    w = lax.axis_index("wave")
    t = lax.axis_index("tile")

    loads = [
        pltpu.make_async_copy(cls, cbuf, in_sem.at[0]),
        pltpu.make_async_copy(cond, cond_s, in_sem.at[1]),
        pltpu.make_async_copy(warm.at[0], xbuf, in_sem.at[2]),
        pltpu.make_async_copy(wn, wn_s, in_sem.at[3]),
        pltpu.make_async_copy(wt, wt_s, in_sem.at[4]),
        pltpu.make_async_copy(srow, srow_s, in_sem.at[5]),
        pltpu.make_async_copy(scol, scol_s, in_sem.at[6]),
        pltpu.make_async_copy(erow, ebuf, in_sem.at[7]),
    ]
    for load in loads:
        load.start()

    below = lax.rem(t + 1, TILES)
    above = lax.rem(t + TILES - 1, TILES)
    group = t // 8
    place = lax.rem(t, 8)
    row_peers = [group * 8 + lax.rem(place + k, 8) for k in range(1, 8)]
    col_peers = [lax.rem(t + 8 * k, TILES) for k in range(1, 4)]
    wave_peers = [lax.rem(w + k, WAVES) for k in range(1, WAVES)]
    barrier = pltpu.get_barrier_semaphore()
    for peer in [below, above] + row_peers + col_peers:
        pl.semaphore_signal(barrier, inc=1, device_id=(w, peer), device_id_type=MESH)
    for peer in wave_peers:
        pl.semaphore_signal(barrier, inc=1, device_id=(peer, t), device_id_type=MESH)

    loads[0].wait()
    loads[1].wait()
    classes = cbuf[...]
    sigma = jnp.full((ROWS, COLS), cond_s[0], jnp.float32)
    for i in range(1, 8):
        sigma = jnp.where(classes == i, cond_s[i], sigma)
    for load in loads[2:]:
        load.wait()
    upper = lax.broadcasted_iota(jnp.int32, (8, COLS), 0) < 4
    upper_half = lax.broadcasted_iota(jnp.int32, (8, COLS // 2), 0) < 4
    half = COLS // 2
    halo_out[0, :, :COLS] = jnp.where(upper, xbuf[0, 0:8, :], pltpu.roll(xbuf[1, 0:8, :], 4, 0))
    halo_out[0, :, COLS:] = jnp.where(upper_half, sigma[0:8, :half], pltpu.roll(sigma[0:8, half:], 4, 0))
    halo_out[1, :, :COLS] = jnp.where(upper, pltpu.roll(xbuf[1, 24:32, :], 4, 0), xbuf[0, 24:32, :])
    halo_out[1, :, COLS:] = jnp.where(upper_half, pltpu.roll(sigma[24:32, half:], 4, 0), sigma[24:32, :half])

    pl.semaphore_wait(barrier, 2 + 7 + 3 + 15)

    def remote(src, dst, send, recv, device):
        return pltpu.make_async_remote_copy(
            src_ref=src, dst_ref=dst, send_sem=send, recv_sem=recv, device_id=device, device_id_type=MESH
        )

    halos = [
        remote(halo_out.at[0], halo_in.at[0], halo_send.at[0], halo_recv.at[0], (w, above)),
        remote(halo_out.at[1], halo_in.at[1], halo_send.at[1], halo_recv.at[1], (w, below)),
    ]
    for copy in halos:
        copy.start()
    for copy in halos:
        copy.wait_recv()

    from_below = halo_in[0]
    from_above = halo_in[1]
    sig_lo = jnp.where(upper_half, from_below[:, COLS:], from_above[:, COLS:])
    sig_hi = pltpu.roll(jnp.where(upper_half, from_above[:, COLS:], from_below[:, COLS:]), 4, 0)
    sig = jnp.concatenate([sigma, jnp.concatenate([sig_lo, sig_hi], axis=1)], axis=0)
    rim = (
        jnp.where(upper, from_below[:, :COLS], from_above[:, :COLS]),
        pltpu.roll(jnp.where(upper, from_above[:, :COLS], from_below[:, :COLS]), 4, 0),
    )

    ext_row = lax.broadcasted_iota(jnp.int32, (EXT, COLS), 0)
    col = lax.broadcasted_iota(jnp.int32, (EXT, COLS), 1)
    closed = jnp.where(t == TILES - 1, ROWS - 1, -1)
    closed_top = jnp.where(t == 0, EXT - 1, -1)

    def down(v):
        return pltpu.roll(v, EXT - 1, 0)

    def up(v):
        return pltpu.roll(v, 1, 0)

    def right(v):
        return pltpu.roll(v, COLS - 1, 1)

    def left(v):
        return pltpu.roll(v, 1, 1)

    face_down = harmonic(sig, down(sig))
    face_down = jnp.where((ext_row == closed) | (ext_row == closed_top), 0.0, face_down)
    face_up = up(face_down)
    last = col == COLS - 1
    face_right = jnp.where(last, 0.0, harmonic(sig, right(sig)))
    face_left = left(face_right)
    k = wn_s[0]
    diag = face_up + face_down + face_left + face_right + jnp.where(last, sig, 0.0) + (k * k) * sig
    inv = 1.0 / diag
    a_up = face_up * inv
    a_down = face_down * inv
    a_left = face_left * inv
    a_right = face_right * inv

    def apply(v):
        return a_up * up(v) + a_down * down(v) + a_left * left(v) + a_right * right(v)

    global_row = jnp.where(ext_row < ROWS + 4, ext_row, ext_row - EXT) + t * ROWS
    d_own = diag[:ROWS]

    def fold(product):
        total = product[:, :LANES]
        for j in range(1, COLS // LANES):
            total = total + product[:, j * LANES:(j + 1) * LANES]
        return jnp.sum(total, axis=0, keepdims=True)

    lane = lax.broadcasted_iota(jnp.int32, (1, LANES), 1)
    vectors = []
    moments = []
    for s in range(2):
        x = jnp.concatenate([xbuf[s], rim[s]], axis=0)
        q = jnp.where((global_row == srow_s[s]) & (col == scol_s[s]), SOURCE_STRENGTH, 0.0)
        v0 = q * inv - x + apply(x)
        v1 = apply(v0)
        v2 = apply(v1)
        v3 = apply(v2)[:ROWS]
        v0, v1, v2 = v0[:ROWS], v1[:ROWS], v2[:ROWS]
        d0, d1, d2 = d_own * v0, d_own * v1, d_own * v2
        moments += [fold(d0 * v0), fold(d0 * v1), fold(d1 * v1), fold(d1 * v2), fold(d2 * v2), fold(d2 * v3)]
        vectors.append((xbuf[s], v0, v1, v2))

    electrode = ebuf[...].reshape(1, 64)
    electrode = jnp.concatenate([electrode, electrode], axis=1)
    here = lax.broadcasted_iota(jnp.int32, (ROWS, LANES), 0) + t * ROWS == electrode
    low = lane < 64
    surface = []
    for i in range(4):
        both = jnp.where(low, vectors[0][i][:, 0:1], vectors[1][i][:, 0:1])
        surface.append(jnp.sum(jnp.where(here, both, 0.0), axis=0, keepdims=True))

    pack_x[...] = jnp.concatenate(moments + surface, axis=0)
    copies_x = [
        remote(pack_x, slots_x.at[i], x_send.at[i], x_recv.at[i], (w, peer)) for i, peer in enumerate(row_peers)
    ]
    for copy in copies_x:
        copy.start()
    total = pack_x[...]
    for i, copy in enumerate(copies_x):
        copy.wait_recv()
        total = total + slots_x[i]
    pack_y[...] = total
    copies_y = [
        remote(pack_y, slots_y.at[i], y_send.at[i], y_recv.at[i], (w, peer)) for i, peer in enumerate(col_peers)
    ]
    for copy in copies_y:
        copy.start()
    for i, copy in enumerate(copies_y):
        copy.wait_recv()
        total = total + slots_y[i]
    dots = jnp.sum(total, axis=1, keepdims=True)

    weight = wt_s[0]
    coefs = []
    for s in range(2):
        nu = [jnp.broadcast_to(dots[6 * s + m:6 * s + m + 1], (1, LANES)) for m in range(6)]
        mu = [nu[m] - nu[m + 1] for m in range(5)]
        gamma0 = nu[0]
        alpha0 = gamma0 / mu[0]
        za, zb = 1.0 - alpha0, alpha0
        gamma1 = za * za * nu[0] + 2.0 * za * zb * nu[1] + zb * zb * nu[2]
        beta0 = gamma1 / gamma0
        pa, pb = za + beta0, zb
        curve1 = pa * pa * mu[0] + 2.0 * pa * pb * mu[1] + pb * pb * mu[2]
        alpha1 = gamma1 / curve1
        ya, yb, yc = za - alpha1 * pa, zb - alpha1 * (pb - pa), alpha1 * pb
        gamma2 = (
            ya * ya * nu[0] + yb * yb * nu[2] + yc * yc * nu[4]
            + 2.0 * (ya * yb * nu[1] + ya * yc * nu[2] + yb * yc * nu[3])
        )
        beta1 = gamma2 / gamma1
        ra, rb, rc = ya + beta1 * pa, yb + beta1 * pb, yc
        curve2 = (
            ra * ra * mu[0] + rb * rb * mu[2] + rc * rc * mu[4]
            + 2.0 * (ra * rb * mu[1] + ra * rc * mu[2] + rb * rc * mu[3])
        )
        alpha2 = gamma2 / curve2
        coefs.append((
            jnp.full((1, LANES), weight, jnp.float32),
            weight * (alpha0 + alpha1 * pa + alpha2 * ra),
            weight * (alpha1 * pb + alpha2 * rb),
            weight * (alpha2 * rc),
        ))

    low_rows = lax.broadcasted_iota(jnp.int32, (ROWS, LANES), 1) < 64
    for j in range(COLS // LANES):
        part = []
        for s in range(2):
            acc = vectors[s][0][:, j * LANES:(j + 1) * LANES] * coefs[s][0]
            for i in range(1, 4):
                acc = acc + vectors[s][i][:, j * LANES:(j + 1) * LANES] * coefs[s][i]
            part.append(acc)
        chunks[2 * j] = jnp.where(low_rows, part[0], pltpu.roll(part[1], 64, 1))
        chunks[2 * j + 1] = jnp.where(low_rows, pltpu.roll(part[0], 64, 1), part[1])

    def owner(offset):
        return lax.rem(w + 2 * WAVES - offset, WAVES)

    copies_first = [
        remote(
            chunks.at[owner(o)], got_first.at[i], first_send.at[i], first_recv.at[i],
            (lax.rem(w + 2 * WAVES + c - o, WAVES), t),
        )
        for i, (c, o) in enumerate(FIRST_LIST)
    ]
    for copy in copies_first:
        copy.start()

    mine[...] = sum(
        surface_total * jnp.where(low, coefs[0][i], coefs[1][i])
        for i, surface_total in enumerate([total[12 + i:13 + i] for i in range(4)])
    )
    copies_r = [
        remote(mine, slots_r.at[i], r_send.at[i], r_recv.at[i], (peer, t)) for i, peer in enumerate(wave_peers)
    ]
    for copy in copies_r:
        copy.start()

    copies_second = []
    for j, c in enumerate(SECOND_LIST):
        acc = chunks[owner(c)]
        for i, (cc, o) in enumerate(FIRST_LIST):
            if cc == c:
                copies_first[i].wait_recv()
                acc = acc + got_first[i]
        sums[j] = acc
        copy = remote(
            sums.at[j], got_second.at[j], second_send.at[j], second_recv.at[j], (owner(c), t)
        )
        copy.start()
        copies_second.append(copy)

    out_r = mine[...]
    for i, copy in enumerate(copies_r):
        copy.wait_recv()
        out_r = out_r + slots_r[i]
    read[0:1, :] = out_r[:, :64]
    read[1:2, :] = out_r[:, 64:]

    acc = chunks[w]
    for i, (c, o) in enumerate(FIRST_LIST):
        if c == 0:
            copies_first[i].wait_recv()
            acc = acc + got_first[i]
    for j, copy in enumerate(copies_second):
        copy.wait_recv()
        acc = acc + got_second[j]
    pot[0] = acc[:, :64]
    pot[1] = acc[:, 64:]

    for copy in halos + copies_x + copies_y + copies_first + copies_r + copies_second:
        copy.wait_send()


def shards(warm, cls, cond, wn, wt, srow, scol, erow):
    f32 = jnp.float32
    dma = pltpu.SemaphoreType.DMA
    n_first, n_second = len(FIRST_LIST), len(SECOND_LIST)
    return pl.pallas_call(
        kernel,
        out_shape=(
            jax.ShapeDtypeStruct((2, ROWS, COLS // WAVES), f32),
            jax.ShapeDtypeStruct((2, 64), f32),
        ),
        in_specs=[pl.BlockSpec(memory_space=pl.ANY)] * 8,
        out_specs=[pl.BlockSpec(memory_space=pltpu.VMEM)] * 2,
        scratch_shapes=[
            pltpu.VMEM((2, ROWS, COLS), f32),
            pltpu.VMEM((ROWS, COLS), jnp.int32),
            pltpu.VMEM((64,), jnp.int32),
            pltpu.SMEM((8,), f32),
            pltpu.SMEM((1,), f32),
            pltpu.SMEM((1,), f32),
            pltpu.SMEM((2,), jnp.int32),
            pltpu.SMEM((2,), jnp.int32),
            pltpu.VMEM((2, 8, COLS + COLS // 2), f32),
            pltpu.VMEM((2, 8, COLS + COLS // 2), f32),
            pltpu.VMEM((16, LANES), f32),
            pltpu.VMEM((16, LANES), f32),
            pltpu.VMEM((7, 16, LANES), f32),
            pltpu.VMEM((3, 16, LANES), f32),
            pltpu.VMEM((WAVES, ROWS, LANES), f32),
            pltpu.VMEM((n_first, ROWS, LANES), f32),
            pltpu.VMEM((n_second, ROWS, LANES), f32),
            pltpu.VMEM((n_second, ROWS, LANES), f32),
            pltpu.VMEM((1, LANES), f32),
            pltpu.VMEM((WAVES - 1, 1, LANES), f32),
            dma((8,)),
            dma((2,)), dma((2,)),
            dma((7,)), dma((7,)),
            dma((3,)), dma((3,)),
            dma((n_first,)), dma((n_first,)),
            dma((n_second,)), dma((n_second,)),
            dma((WAVES - 1,)), dma((WAVES - 1,)),
        ],
        compiler_params=pltpu.CompilerParams(
            collective_id=0, has_side_effects=True, vmem_limit_bytes=40 * 1024 * 1024
        ),
    )(warm, cls, cond, wn, wt, srow, scol, erow)


def solution(mesh):
    return jax.shard_map(
        shards,
        mesh=mesh,
        in_specs=(
            P("wave", None, "tile", None), P("tile", None), P(), P("wave"), P("wave"), P(), P(), P(),
        ),
        out_specs=(P(None, "tile", "wave"), P()),
        check_vma=False,
    )
```

time: 509 us -> 42.7 us (0.08)
  the two profiles are of different devices: /device:TPU:2 before, /device:TPU:32 now
where the time goes in v1:
time: 42.7 us; the launch traced here: 42.5 us
  Pallas kernels  37.4 us (88%)
  local copies, waits for them, and re-layouts  3.04 us (7%)
  between operations  2.04 us (5%)
    pallas_call x1, Pallas kernels, shards(): pl.pallas_call(kernel, out_shape=(jax.ShapeDtypeStruct((2, ROWS, COLS //...  37.4 us
    unnamed x14, local copies, waits for them, and re-layouts  3.04 us

profile of v1, /device:TPU:32, one launch (start us, length us, event | category | flops | bytes accessed | tf_op | source)
XLA Modules:
  0.0 42.5 jit_solution(11635555649441881950)
XLA Ops:
  0.6 0.0 copy-start.5
  1.3 0.0 copy-start.2
  1.3 0.0 copy-start.3
  1.3 0.0 copy-start.4
  2.0 0.0 copy-done.5
  2.0 0.0 copy-done.2
  2.0 0.0 copy-done.3
  2.0 0.0 copy-done.4
  2.0 0.0 copy-start
  2.1 0.9 %copy-done = f32[1,2,32,1024]{3,2,1,0:T(8,128)S(1)} copy-done((f32[1,2,32,1024]{3,2,1,0:T(8,128)S(1)}, f32[1,2,32,1024]{3,2,1,0:T(8,128)}, u32[]{:S(2)}) %copy-start) | copy-done | bytes 262168
  3.0 0.0 copy-start.1
  3.0 0.9 %copy-done.1 = s32[32,1024]{1,0:T(8,128)S(1)} copy-done((s32[32,1024]{1,0:T(8,128)S(1)}, s32[32,1024]{1,0:T(8,128)}, u32[]{:S(2)}) %copy-start.1) | copy-done | bytes 131096
  3.9 37.4 %shard_map.95 = (f32[2,32,64]{2,1,0:T(8,128)S(1)}, f32[2,64]{1,0:T(2,128)S(1)}) custom-call(f32[1,2,32,1024]{3,2,1,0:T(8,128)S(1)} %copy-done, s32[32,1024]{1,0:T(8,128)S(1)} %copy-done.1, f32[8]{0:T(128)S(1)} %copy-done.2, f32[1]{0:T(128)S(6)} %copy.12.wn, f32[1]{0:T(128)S(6)} %copy.13.wt, s32[2]{0:T(128)S(1)} %copy-done.3, s32[2]{0:T(128)S(1)} %copy-done.4, ...), custom_call_target="tpu_custom_call" | custom-call | tf_op jit(solution)/shard_map/pallas_call | solution.py:303
  41.3 0.6 %copy.14 = f32[2,32,64]{2,1,0:T(8,128)} copy(f32[2,32,64]{2,1,0:T(8,128)S(1)} %get-tuple-element.4) | data formatting | bytes 32768
  42.0 0.6 %copy.15 = f32[2,64]{1,0:T(2,128)} copy(f32[2,64]{1,0:T(2,128)S(1)} %get-tuple-element.5) | data formatting | bytes 1024
Async XLA Ops:
  0.6 1.4 %copy-start.5 = (s32[64]{0:T(128)S(1)}, s32[64]{0:T(128)}, u32[]{:S(2)}) copy-start(s32[64]{0:T(128)} %erow.1) | copy-start | bytes 772
  1.3 0.7 %copy-start.2 = (f32[8]{0:T(128)S(1)}, f32[8]{0:T(128)}, u32[]{:S(2)}) copy-start(f32[8]{0:T(128)} %cond.1) | copy-start | bytes 100
  1.3 0.7 %copy-start.3 = (s32[2]{0:T(128)S(1)}, s32[2]{0:T(128)}, u32[]{:S(2)}) copy-start(s32[2]{0:T(128)} %srow.1) | copy-start | bytes 28
  1.3 0.7 %copy-start.4 = (s32[2]{0:T(128)S(1)}, s32[2]{0:T(128)}, u32[]{:S(2)}) copy-start(s32[2]{0:T(128)} %scol.1) | copy-start | bytes 28
  2.0 1.0 %copy-start = (f32[1,2,32,1024]{3,2,1,0:T(8,128)S(1)}, f32[1,2,32,1024]{3,2,1,0:T(8,128)}, u32[]{:S(2)}) copy-start(f32[1,2,32,1024]{3,2,1,0:T(8,128)} %warm.1) | copy-start | bytes 786436
  3.0 0.9 %copy-start.1 = (s32[32,1024]{1,0:T(8,128)S(1)}, s32[32,1024]{1,0:T(8,128)}, u32[]{:S(2)}) copy-start(s32[32,1024]{1,0:T(8,128)} %cls.1) | copy-start | bytes 393220

commit v2 on v1

v2 whole, which is shorter than its diff:
```python
import jax
import jax.numpy as jnp
from jax import lax
from jax.experimental import pallas as pl
from jax.experimental.pallas import tpu as pltpu
from jax.sharding import PartitionSpec as P

SOURCE_STRENGTH = 50.0
MESH = pl.DeviceIdType.MESH

WAVES = 16
TILES = 32
ROWS = 32
COLS = 1024
LANES = 128
HALF = COLS // 2

FIRST = {7: (6, 8), -7: (-6,), 4: (3, 5), -4: (-3, -5), 2: (1,), -2: (-1,)}
FIRST_LIST = [(c, o) for c, offsets in FIRST.items() for o in offsets]
SECOND_LIST = list(FIRST)

STEPS = sorted(
    [(a, b, c) for a in range(4) for b in range(4) for c in range(2) if (a, b, c) != (0, 0, 0)],
    key=lambda s: -(min(s[0], 4 - s[0]) + min(s[1], 4 - s[1])),
)
NEAR = [s for s in STEPS if min(s[0], 4 - s[0]) + min(s[1], 4 - s[1]) <= 1]
FAR = [s for s in STEPS if min(s[0], 4 - s[0]) + min(s[1], 4 - s[1]) == 2 and s[2] == 0]


def harmonic(a, b):
    return 2.0 * a * b / (a + b)


def right(v):
    return pltpu.roll(v, COLS - 1, 1)


def left(v):
    return pltpu.roll(v, 1, 1)


def kernel(
    warm, cls, cond, wn, wt, srow, scol, erow,
    pot, read,
    xbuf, cbuf, ebuf, cond_s, wn_s, wt_s, srow_s, scol_s,
    halo_out, halo_in, packet, slots,
    chunks, got_first, sums, got_second, mine, slots_r,
    in_sem, halo_send, halo_recv, tile_send, tile_recv,
    first_send, first_recv, second_send, second_recv, r_send, r_recv,
    known,
):
    w = lax.axis_index("wave")
    t = lax.axis_index("tile")

    loads = [
        pltpu.make_async_copy(cls, cbuf, in_sem.at[0]),
        pltpu.make_async_copy(cond, cond_s, in_sem.at[1]),
        pltpu.make_async_copy(warm.at[0], xbuf, in_sem.at[2]),
        pltpu.make_async_copy(wn, wn_s, in_sem.at[3]),
        pltpu.make_async_copy(wt, wt_s, in_sem.at[4]),
        pltpu.make_async_copy(srow, srow_s, in_sem.at[5]),
        pltpu.make_async_copy(scol, scol_s, in_sem.at[6]),
        pltpu.make_async_copy(erow, ebuf, in_sem.at[7]),
    ]
    for load in loads:
        load.start()

    below = lax.rem(t + 1, TILES)
    above = lax.rem(t + TILES - 1, TILES)
    t_y, t_x, t_core = t // 8, lax.rem(t // 2, 4), lax.rem(t, 2)

    def tile_peer(step):
        dy, dx, dc = step
        return (w, lax.rem(t_y + dy, 4) * 8 + lax.rem(t_x + dx, 4) * 2 + lax.rem(t_core + dc, 2))

    def wave_peer(k):
        return (lax.rem(w + 2 * WAVES + k, WAVES), t)

    def tell(semaphore, peers):
        for peer in peers:
            pl.semaphore_signal(semaphore, inc=1, device_id=peer, device_id_type=MESH)

    near = [(w, below), (w, above)] + [tile_peer(s) for s in NEAR] + [wave_peer(1), wave_peer(-1)]
    middle = [tile_peer(s) for s in FAR] + [wave_peer(2), wave_peer(-2)]
    far = [wave_peer(4), wave_peer(-4)]
    barrier = pltpu.get_barrier_semaphore()
    tell(barrier, near)

    loads[0].wait()
    loads[1].wait()
    classes = cbuf[...]
    sigma = jnp.full((ROWS, COLS), cond_s[0], jnp.float32)
    for i in range(1, 8):
        sigma = jnp.where(classes == i, cond_s[i], sigma)
    for load in loads[2:]:
        load.wait()
    upper = lax.broadcasted_iota(jnp.int32, (8, COLS), 0) < 4
    upper_half = lax.broadcasted_iota(jnp.int32, (8, HALF), 0) < 4
    halo_out[0, :, :COLS] = jnp.where(upper, xbuf[0, 0:8, :], pltpu.roll(xbuf[1, 0:8, :], 4, 0))
    halo_out[0, :, COLS:] = jnp.where(upper_half, sigma[0:8, :HALF], pltpu.roll(sigma[0:8, HALF:], 4, 0))
    halo_out[1, :, :COLS] = jnp.where(upper, pltpu.roll(xbuf[1, 24:32, :], 4, 0), xbuf[0, 24:32, :])
    halo_out[1, :, COLS:] = jnp.where(upper_half, pltpu.roll(sigma[24:32, HALF:], 4, 0), sigma[24:32, :HALF])

    pl.semaphore_wait(barrier, len(near))

    def remote(src, dst, send, recv, device):
        return pltpu.make_async_remote_copy(
            src_ref=src, dst_ref=dst, send_sem=send, recv_sem=recv, device_id=device, device_id_type=MESH
        )

    halos = [
        remote(halo_out.at[0], halo_in.at[0], halo_send.at[0], halo_recv.at[0], (w, above)),
        remote(halo_out.at[1], halo_in.at[1], halo_send.at[1], halo_recv.at[1], (w, below)),
    ]
    for copy in halos:
        copy.start()
    tell(known.at[0], near)

    k = wn_s[0]

    def stencil(sig, cell_row, up, down, closed):
        shape = sig.shape
        row = lax.broadcasted_iota(jnp.int32, shape, 0)
        col = lax.broadcasted_iota(jnp.int32, shape, 1)
        last = col == COLS - 1
        face_down = harmonic(sig, down(sig, 0))
        face_up = harmonic(sig, up(sig, 0))
        if closed is not None:
            face_down = jnp.where(closed[1](row), 0.0, face_down)
            face_up = jnp.where(closed[0](row), 0.0, face_up)
        face_right = jnp.where(last, 0.0, harmonic(sig, right(sig)))
        face_left = left(face_right)
        diag = face_up + face_down + face_left + face_right + jnp.where(last, sig, 0.0) + (k * k) * sig
        inv = 1.0 / diag
        a_up, a_down, a_left, a_right = face_up * inv, face_down * inv, face_left * inv, face_right * inv

        def apply(v, tag):
            return a_up * up(v, tag) + a_down * down(v, tag) + a_left * left(v) + a_right * right(v)

        def chain(x, s):
            q = jnp.where((cell_row(row) + t * ROWS == srow_s[s]) & (col == scol_s[s]), SOURCE_STRENGTH, 0.0)
            v0 = q * inv - x + apply(x, (s, 0))
            v1 = apply(v0, (s, 1))
            v2 = apply(v1, (s, 2))
            return v0, v1, v2, apply(v2, (s, 3))

        return diag, chain

    def fold(product):
        total = product[:, :LANES]
        for j in range(1, COLS // LANES):
            total = total + product[:, j * LANES:(j + 1) * LANES]
        return jnp.sum(total, axis=0, keepdims=True)

    def moments(d, v0, v1, v2, v3):
        d0, d1, d2 = d * v0, d * v1, d * v2
        return [fold(a * b) for a, b in ((d0, v0), (d0, v1), (d1, v1), (d1, v2), (d2, v2), (d2, v3))]

    diag, chain = stencil(
        sigma,
        lambda row: row,
        lambda v, tag: pltpu.roll(v, 1, 0),
        lambda v, tag: pltpu.roll(v, ROWS - 1, 0),
        None,
    )
    inner = [chain(xbuf[s], s) for s in range(2)]
    inner_moments = [moments(diag[8:24], *[v[8:24] for v in inner[s]]) for s in range(2)]

    electrode = ebuf[...].reshape(1, 64)
    electrode = jnp.concatenate([electrode, electrode], axis=1)
    here = lax.broadcasted_iota(jnp.int32, (ROWS, LANES), 0) + t * ROWS == electrode

    for copy in halos:
        copy.wait_recv()
    pl.semaphore_wait(known.at[0], len(near))
    tell(known.at[1], middle)

    from_below = halo_in[0]
    from_above = halo_in[1]
    sig_lo = jnp.where(upper_half, from_below[:, COLS:], from_above[:, COLS:])
    sig_hi = pltpu.roll(jnp.where(upper_half, from_above[:, COLS:], from_below[:, COLS:]), 4, 0)
    rim_sigma = jnp.concatenate([sig_lo, sig_hi], axis=1)
    rim = (
        jnp.where(upper, from_below[:, :COLS], from_above[:, :COLS]),
        pltpu.roll(jnp.where(upper, from_above[:, :COLS], from_below[:, :COLS]), 4, 0),
    )
    own = {0: sigma}
    for s in range(2):
        own[(s, 0)] = xbuf[s]
        for i in range(3):
            own[(s, i + 1)] = inner[s][i]

    def strip(v, middle_rows):
        return jnp.concatenate([v[24:32], middle_rows, v[0:8]], axis=0)

    def strip_up(v, tag):
        return pltpu.roll(jnp.concatenate([own[tag][16:24], v], axis=0), 1, 0)[8:]

    def strip_down(v, tag):
        return pltpu.roll(jnp.concatenate([v, own[tag][8:16]], axis=0), 31, 0)[:24]

    bottom = jnp.where(t == TILES - 1, 0, 100)
    top = jnp.where(t == 0, 0, 100)
    diag_s, chain_s = stencil(
        strip(sigma, rim_sigma),
        lambda row: jnp.where(row < 12, row + 24, row - 16),
        strip_up,
        strip_down,
        (
            lambda row: (row == 8 + bottom) | (row == 16 + top),
            lambda row: (row == 7 + bottom) | (row == 15 + top),
        ),
    )
    del diag, chain
    vectors = []
    rows = []
    d_edge = jnp.concatenate([diag_s[16:24], diag_s[0:8]], axis=0)
    for s in range(2):
        outer = chain_s(strip(xbuf[s], rim[s]), s)
        edge = [jnp.concatenate([v[16:24], v[0:8]], axis=0) for v in outer]
        rows += [a + b for a, b in zip(inner_moments[s], moments(d_edge, *edge))]
        vectors.append(
            [xbuf[s]]
            + [jnp.concatenate([e[0:8], v[8:24], e[8:16]], axis=0) for v, e in zip(inner[s][:3], edge[:3])]
        )

    lane = lax.broadcasted_iota(jnp.int32, (1, LANES), 1)
    low = lane < 64
    surface = []
    for i in range(4):
        both = jnp.where(low, vectors[0][i][:, 0:1], vectors[1][i][:, 0:1])
        surface.append(jnp.sum(jnp.where(here, both, 0.0), axis=0, keepdims=True))

    dots = jnp.sum(jnp.concatenate(rows, axis=0), axis=1, keepdims=True)
    eye = lax.broadcasted_iota(jnp.int32, (12, LANES), 0) == lax.broadcasted_iota(jnp.int32, (12, LANES), 1)
    moment_row = jnp.sum(jnp.where(eye, dots, 0.0), axis=0, keepdims=True)
    packet[...] = jnp.concatenate([moment_row] + surface + [jnp.zeros((3, LANES), jnp.float32)], axis=0)
    pl.semaphore_wait(known.at[1], len(middle))
    copies_t = [
        remote(packet, slots.at[i], tile_send, tile_recv, tile_peer(step)) for i, step in enumerate(STEPS)
    ]
    for copy in copies_t:
        copy.start()
    tell(known.at[2], far)
    every = remote(slots, slots, tile_send, tile_recv, (w, below))
    every.wait_recv()
    total = packet[...] + jnp.sum(slots[...], axis=0)
    pl.semaphore_wait(known.at[2], len(far))

    weight = wt_s[0]
    coefs = []
    for s in range(2):
        nu = [jnp.broadcast_to(total[0:1, 6 * s + m:6 * s + m + 1], (1, LANES)) for m in range(6)]
        mu = [nu[m] - nu[m + 1] for m in range(5)]
        gamma0 = nu[0]
        alpha0 = gamma0 / mu[0]
        za, zb = 1.0 - alpha0, alpha0
        gamma1 = za * za * nu[0] + 2.0 * za * zb * nu[1] + zb * zb * nu[2]
        beta0 = gamma1 / gamma0
        pa, pb = za + beta0, zb
        curve1 = pa * pa * mu[0] + 2.0 * pa * pb * mu[1] + pb * pb * mu[2]
        alpha1 = gamma1 / curve1
        ya, yb, yc = za - alpha1 * pa, zb - alpha1 * (pb - pa), alpha1 * pb
        gamma2 = (
            ya * ya * nu[0] + yb * yb * nu[2] + yc * yc * nu[4]
            + 2.0 * (ya * yb * nu[1] + ya * yc * nu[2] + yb * yc * nu[3])
        )
        beta1 = gamma2 / gamma1
        ra, rb, rc = ya + beta1 * pa, yb + beta1 * pb, yc
        curve2 = (
            ra * ra * mu[0] + rb * rb * mu[2] + rc * rc * mu[4]
            + 2.0 * (ra * rb * mu[1] + ra * rc * mu[2] + rb * rc * mu[3])
        )
        alpha2 = gamma2 / curve2
        coefs.append((
            jnp.full((1, LANES), weight, jnp.float32),
            weight * (alpha0 + alpha1 * pa + alpha2 * ra),
            weight * (alpha1 * pb + alpha2 * rb),
            weight * (alpha2 * rc),
        ))

    low_rows = lax.broadcasted_iota(jnp.int32, (ROWS, LANES), 1) < 64
    for j in range(COLS // LANES):
        part = []
        for s in range(2):
            acc = vectors[s][0][:, j * LANES:(j + 1) * LANES] * coefs[s][0]
            for i in range(1, 4):
                acc = acc + vectors[s][i][:, j * LANES:(j + 1) * LANES] * coefs[s][i]
            part.append(acc)
        chunks[2 * j] = jnp.where(low_rows, part[0], pltpu.roll(part[1], 64, 1))
        chunks[2 * j + 1] = jnp.where(low_rows, pltpu.roll(part[0], 64, 1), part[1])

    copies_first = [
        remote(
            chunks.at[wave_peer(-o)[0]], got_first.at[i], first_send.at[i], first_recv.at[i], wave_peer(c - o)
        )
        for i, (c, o) in enumerate(FIRST_LIST)
    ]
    for copy in copies_first:
        copy.start()

    mine[...] = sum(total[1 + i:2 + i] * jnp.where(low, coefs[0][i], coefs[1][i]) for i in range(4))
    copies_r = [
        remote(mine, slots_r.at[i], r_send, r_recv, wave_peer(i + 1)) for i in range(WAVES - 1)
    ]
    for copy in copies_r:
        copy.start()

    copies_second = []
    for j, c in enumerate(SECOND_LIST):
        acc = chunks[wave_peer(-c)[0]]
        for i, (cc, o) in enumerate(FIRST_LIST):
            if cc == c:
                copies_first[i].wait_recv()
                acc = acc + got_first[i]
        sums[j] = acc
        copy = remote(sums.at[j], got_second.at[j], second_send.at[j], second_recv.at[j], wave_peer(-c))
        copy.start()
        copies_second.append(copy)
    every_r = remote(slots_r, slots_r, r_send, r_recv, wave_peer(1))

    acc = chunks[w]
    for j in reversed(range(len(SECOND_LIST))):
        copies_second[j].wait_recv()
        acc = acc + got_second[j]
    pot[0] = acc[:, :64]
    pot[1] = acc[:, 64:]

    every_r.wait_recv()
    out_r = mine[...] + jnp.sum(slots_r[...], axis=0)
    read[0:1, :] = out_r[:, :64]
    read[1:2, :] = out_r[:, 64:]

    for copy in halos + [every, every_r] + copies_first + copies_second:
        copy.wait_send()


def shards(warm, cls, cond, wn, wt, srow, scol, erow):
    f32 = jnp.float32
    dma = pltpu.SemaphoreType.DMA
    n_first, n_second = len(FIRST_LIST), len(SECOND_LIST)
    return pl.pallas_call(
        kernel,
        out_shape=(
            jax.ShapeDtypeStruct((2, ROWS, COLS // WAVES), f32),
            jax.ShapeDtypeStruct((2, 64), f32),
        ),
        in_specs=[pl.BlockSpec(memory_space=pltpu.HBM)] * 8,
        out_specs=[pl.BlockSpec(memory_space=pltpu.VMEM)] * 2,
        scratch_shapes=[
            pltpu.VMEM((2, ROWS, COLS), f32),
            pltpu.VMEM((ROWS, COLS), jnp.int32),
            pltpu.VMEM((64,), jnp.int32),
            pltpu.SMEM((8,), f32),
            pltpu.SMEM((1,), f32),
            pltpu.SMEM((1,), f32),
            pltpu.SMEM((2,), jnp.int32),
            pltpu.SMEM((2,), jnp.int32),
            pltpu.VMEM((2, 8, COLS + HALF), f32),
            pltpu.VMEM((2, 8, COLS + HALF), f32),
            pltpu.VMEM((8, LANES), f32),
            pltpu.VMEM((TILES - 1, 8, LANES), f32),
            pltpu.VMEM((WAVES, ROWS, LANES), f32),
            pltpu.VMEM((n_first, ROWS, LANES), f32),
            pltpu.VMEM((n_second, ROWS, LANES), f32),
            pltpu.VMEM((n_second, ROWS, LANES), f32),
            pltpu.VMEM((1, LANES), f32),
            pltpu.VMEM((WAVES - 1, 1, LANES), f32),
            dma((8,)),
            dma((2,)), dma((2,)),
            dma, dma,
            dma((n_first,)), dma((n_first,)),
            dma((n_second,)), dma((n_second,)),
            dma, dma,
            pltpu.SemaphoreType.REGULAR((3,)),
        ],
        compiler_params=pltpu.CompilerParams(
            collective_id=0, has_side_effects=True, vmem_limit_bytes=60 * 1024 * 1024
        ),
    )(warm, cls, cond, wn, wt, srow, scol, erow)


def solution(mesh):
    return jax.shard_map(
        shards,
        mesh=mesh,
        in_specs=(
            P("wave", None, "tile", None), P("tile", None), P(), P("wave"), P("wave"), P(), P(), P(),
        ),
        out_specs=(P(None, "tile", "wave"), P()),
        check_vma=False,
    )
```

time: 42.7 us -> 40.7 us (0.953)
  local copies, waits for them, and re-layouts: 3.04 us -> 1.94 us
  Pallas kernels: 37.4 us -> 36.6 us
    unnamed x14 -> x4, local copies, waits for them, and re-layouts: 3.04 us -> 1.94 us
    pallas_call x1, Pallas kernels: 37.4 us -> 36.6 us  [shards(): pl.pallas_call(kernel, out_shape=(jax.ShapeDtypeStruct((2, ROWS, COLS //...]
where the time goes in v2:
time: 40.7 us; the launch traced here: 40.5 us
  Pallas kernels  36.6 us (90%)
  local copies, waits for them, and re-layouts  1.94 us (5%)
  between operations  1.94 us (5%)
    pallas_call x1, Pallas kernels, shards(): pl.pallas_call(kernel, out_shape=(jax.ShapeDtypeStruct((2, ROWS, COLS //...  36.6 us
    unnamed x4, local copies, waits for them, and re-layouts  1.94 us

profile of v2, /device:TPU:32, one launch (start us, length us, event | category | flops | bytes accessed | tf_op | source)
XLA Modules:
  0.0 40.5 jit_solution(14610790133263295742)
XLA Ops:
  1.9 36.6 %shard_map.95 = (f32[2,32,64]{2,1,0:T(8,128)}, f32[2,64]{1,0:T(2,128)}) custom-call(f32[1,2,32,1024]{3,2,1,0:T(8,128)} %warm.1, s32[32,1024]{1,0:T(8,128)} %cls.1, f32[8]{0:T(128)} %cond.1, f32[1]{0:T(128)S(6)} %copy.12.wn, f32[1]{0:T(128)S(6)} %copy.13.wt, s32[2]{0:T(128)} %srow.1, s32[2]{0:T(128)} %scol.1, s32[64]{0:T(128)} %erow.1), custom_call_target="tpu_custom_call" | custom-call | tf_op jit(solution)/shard_map/pallas_call | solution.py:342
  38.5 0.0 copy-start
  38.6 1.4 %copy.14 = f32[2,32,64]{2,1,0:T(8,128)} copy(f32[2,32,64]{2,1,0:T(8,128)} %get-tuple-element.4) | data formatting | bytes 32768
  39.9 0.0 copy-done
  39.9 0.6 %copy.15 = f32[2,64]{1,0:T(2,128)} copy(f32[2,64]{1,0:T(2,128)S(1)} %copy-done) | data formatting | bytes 1024
Async XLA Ops:
  38.5 1.4 %copy-start = (f32[2,64]{1,0:T(2,128)S(1)}, f32[2,64]{1,0:T(2,128)}, u32[]{:S(2)}) copy-start(f32[2,64]{1,0:T(2,128)} %get-tuple-element.5) | copy-start | bytes 1540

commit v3 on v2

--- a/solution.py
+++ b/solution.py
@@ -13,7 +13,6 @@
 ROWS = 32
 COLS = 1024
 LANES = 128
-HALF = COLS // 2
 
 FIRST = {7: (6, 8), -7: (-6,), 4: (3, 5), -4: (-3, -5), 2: (1,), -2: (-1,)}
 FIRST_LIST = [(c, o) for c, offsets in FIRST.items() for o in offsets]
@@ -43,7 +42,7 @@
     warm, cls, cond, wn, wt, srow, scol, erow,
     pot, read,
     xbuf, cbuf, ebuf, cond_s, wn_s, wt_s, srow_s, scol_s,
-    halo_out, halo_in, packet, slots,
+    halo_c, halo_x, packet, slots, surfaces, slots_e,
     chunks, got_first, sums, got_second, mine, slots_r,
     in_sem, halo_send, halo_recv, tile_send, tile_recv,
     first_send, first_recv, second_send, second_recv, r_send, r_recv,
@@ -86,35 +85,32 @@
     barrier = pltpu.get_barrier_semaphore()
     tell(barrier, near)
 
-    loads[0].wait()
-    loads[1].wait()
-    classes = cbuf[...]
-    sigma = jnp.full((ROWS, COLS), cond_s[0], jnp.float32)
-    for i in range(1, 8):
-        sigma = jnp.where(classes == i, cond_s[i], sigma)
-    for load in loads[2:]:
-        load.wait()
-    upper = lax.broadcasted_iota(jnp.int32, (8, COLS), 0) < 4
-    upper_half = lax.broadcasted_iota(jnp.int32, (8, HALF), 0) < 4
-    halo_out[0, :, :COLS] = jnp.where(upper, xbuf[0, 0:8, :], pltpu.roll(xbuf[1, 0:8, :], 4, 0))
-    halo_out[0, :, COLS:] = jnp.where(upper_half, sigma[0:8, :HALF], pltpu.roll(sigma[0:8, HALF:], 4, 0))
-    halo_out[1, :, :COLS] = jnp.where(upper, pltpu.roll(xbuf[1, 24:32, :], 4, 0), xbuf[0, 24:32, :])
-    halo_out[1, :, COLS:] = jnp.where(upper_half, pltpu.roll(sigma[24:32, HALF:], 4, 0), sigma[24:32, :HALF])
-
-    pl.semaphore_wait(barrier, len(near))
-
     def remote(src, dst, send, recv, device):
         return pltpu.make_async_remote_copy(
             src_ref=src, dst_ref=dst, send_sem=send, recv_sem=recv, device_id=device, device_id_type=MESH
         )
 
+    first, final = pl.ds(0, 8), pl.ds(ROWS - 8, 8)
     halos = [
-        remote(halo_out.at[0], halo_in.at[0], halo_send.at[0], halo_recv.at[0], (w, above)),
-        remote(halo_out.at[1], halo_in.at[1], halo_send.at[1], halo_recv.at[1], (w, below)),
-    ]
+        remote(cls.at[first], halo_c.at[0], halo_send.at[0], halo_recv.at[0], (w, above)),
+        remote(cls.at[final], halo_c.at[1], halo_send.at[1], halo_recv.at[1], (w, below)),
+        remote(warm.at[0, :, first], halo_x.at[0], halo_send.at[2], halo_recv.at[2], (w, above)),
+        remote(warm.at[0, :, final], halo_x.at[1], halo_send.at[3], halo_recv.at[3], (w, below)),
+    ]
+    pl.semaphore_wait(barrier, len(near))
     for copy in halos:
         copy.start()
     tell(known.at[0], near)
+
+    def conductivity(classes):
+        value = jnp.full(classes.shape, cond_s[0], jnp.float32)
+        for i in range(1, 8):
+            value = jnp.where(classes == i, cond_s[i], value)
+        return value
+
+    for load in loads:
+        load.wait()
+    sigma = conductivity(cbuf[...])
 
     k = wn_s[0]
 
@@ -124,10 +120,11 @@
         col = lax.broadcasted_iota(jnp.int32, shape, 1)
         last = col == COLS - 1
         face_down = harmonic(sig, down(sig, 0))
-        face_up = harmonic(sig, up(sig, 0))
-        if closed is not None:
-            face_down = jnp.where(closed[1](row), 0.0, face_down)
-            face_up = jnp.where(closed[0](row), 0.0, face_up)
+        if closed is None:
+            face_up = up(face_down, None)
+        else:
+            face_up = jnp.where(row == closed[0], 0.0, harmonic(sig, up(sig, 0)))
+            face_down = jnp.where(row == closed[1], 0.0, face_down)
         face_right = jnp.where(last, 0.0, harmonic(sig, right(sig)))
         face_left = left(face_right)
         diag = face_up + face_down + face_left + face_right + jnp.where(last, sig, 0.0) + (k * k) * sig
@@ -150,11 +147,15 @@
         total = product[:, :LANES]
         for j in range(1, COLS // LANES):
             total = total + product[:, j * LANES:(j + 1) * LANES]
-        return jnp.sum(total, axis=0, keepdims=True)
+        return total
 
     def moments(d, v0, v1, v2, v3):
         d0, d1, d2 = d * v0, d * v1, d * v2
         return [fold(a * b) for a, b in ((d0, v0), (d0, v1), (d1, v1), (d1, v2), (d2, v2), (d2, v3))]
+
+    sub = lax.broadcasted_iota(jnp.int32, (8, COLS), 0)
+    upper = sub < 4
+    upper_lanes = lax.broadcasted_iota(jnp.int32, (8, LANES), 0) < 4
 
     diag, chain = stencil(
         sigma,
@@ -164,7 +165,15 @@
         None,
     )
     inner = [chain(xbuf[s], s) for s in range(2)]
-    inner_moments = [moments(diag[8:24], *[v[8:24] for v in inner[s]]) for s in range(2)]
+    inner_moments = [
+        [f[8:16] + f[16:24] + jnp.where(upper_lanes, f[24:32], f[0:8]) for f in moments(diag, *inner[s])]
+        for s in range(2)
+    ]
+    own = {0: (sigma[0:8], sigma[24:32])}
+    for s in range(2):
+        own[(s, 0)] = (xbuf[s, 0:8, :], xbuf[s, 24:32, :])
+        for i in range(3):
+            own[(s, i + 1)] = (inner[s][i][0:8], inner[s][i][24:32])
 
     electrode = ebuf[...].reshape(1, 64)
     electrode = jnp.concatenate([electrode, electrode], axis=1)
@@ -175,74 +184,70 @@
     pl.semaphore_wait(known.at[0], len(near))
     tell(known.at[1], middle)
 
-    from_below = halo_in[0]
-    from_above = halo_in[1]
-    sig_lo = jnp.where(upper_half, from_below[:, COLS:], from_above[:, COLS:])
-    sig_hi = pltpu.roll(jnp.where(upper_half, from_above[:, COLS:], from_below[:, COLS:]), 4, 0)
-    rim_sigma = jnp.concatenate([sig_lo, sig_hi], axis=1)
-    rim = (
-        jnp.where(upper, from_below[:, :COLS], from_above[:, :COLS]),
-        pltpu.roll(jnp.where(upper, from_above[:, :COLS], from_below[:, :COLS]), 4, 0),
-    )
-    own = {0: sigma}
+    edge_stencil = [
+        stencil(
+            jnp.where(upper, sigma[0:8], conductivity(halo_c[1])),
+            lambda row: jnp.where(row < 4, row, row - 8),
+            lambda v, tag: pltpu.roll(v, 1, 0),
+            lambda v, tag: pltpu.roll(jnp.where(sub == 4, own[tag][0], v), 7, 0),
+            (jnp.where(t == 0, 0, -1), jnp.where(t == 0, 7, -1)),
+        ),
+        stencil(
+            jnp.where(upper, conductivity(halo_c[0]), sigma[24:32]),
+            lambda row: jnp.where(row < 4, row + 32, row + 24),
+            lambda v, tag: pltpu.roll(jnp.where(sub == 3, own[tag][1], v), 1, 0),
+            lambda v, tag: pltpu.roll(v, 7, 0),
+            (jnp.where(t == TILES - 1, 0, -1), jnp.where(t == TILES - 1, 7, -1)),
+        ),
+    ]
+    edges = []
+    rows = []
     for s in range(2):
-        own[(s, 0)] = xbuf[s]
-        for i in range(3):
-            own[(s, i + 1)] = inner[s][i]
-
-    def strip(v, middle_rows):
-        return jnp.concatenate([v[24:32], middle_rows, v[0:8]], axis=0)
-
-    def strip_up(v, tag):
-        return pltpu.roll(jnp.concatenate([own[tag][16:24], v], axis=0), 1, 0)[8:]
-
-    def strip_down(v, tag):
-        return pltpu.roll(jnp.concatenate([v, own[tag][8:16]], axis=0), 31, 0)[:24]
-
-    bottom = jnp.where(t == TILES - 1, 0, 100)
-    top = jnp.where(t == 0, 0, 100)
-    diag_s, chain_s = stencil(
-        strip(sigma, rim_sigma),
-        lambda row: jnp.where(row < 12, row + 24, row - 16),
-        strip_up,
-        strip_down,
-        (
-            lambda row: (row == 8 + bottom) | (row == 16 + top),
-            lambda row: (row == 7 + bottom) | (row == 15 + top),
-        ),
-    )
-    del diag, chain
-    vectors = []
-    rows = []
-    d_edge = jnp.concatenate([diag_s[16:24], diag_s[0:8]], axis=0)
-    for s in range(2):
-        outer = chain_s(strip(xbuf[s], rim[s]), s)
-        edge = [jnp.concatenate([v[16:24], v[0:8]], axis=0) for v in outer]
-        rows += [a + b for a, b in zip(inner_moments[s], moments(d_edge, *edge))]
-        vectors.append(
-            [xbuf[s]]
-            + [jnp.concatenate([e[0:8], v[8:24], e[8:16]], axis=0) for v, e in zip(inner[s][:3], edge[:3])]
-        )
-
+        block0 = edge_stencil[0][1](jnp.where(upper, own[(s, 0)][0], halo_x[1, s]), s)
+        block1 = edge_stencil[1][1](jnp.where(upper, halo_x[0, s], own[(s, 0)][1]), s)
+        outer = zip(moments(edge_stencil[0][0], *block0), moments(edge_stencil[1][0], *block1))
+        rows += [
+            jnp.sum(a + jnp.where(upper_lanes, b, c), axis=0, keepdims=True)
+            for a, (b, c) in zip(inner_moments[s], outer)
+        ]
+        edges.append((block0, block1))
+
+    dots = jnp.sum(jnp.concatenate(rows, axis=0), axis=1, keepdims=True)
+    eye = lax.broadcasted_iota(jnp.int32, (12, LANES), 0) == lax.broadcasted_iota(jnp.int32, (12, LANES), 1)
+    packet[...] = jnp.sum(jnp.where(eye, dots, 0.0), axis=0, keepdims=True)
+    pl.semaphore_wait(known.at[1], len(middle))
+    peers = [tile_peer(step) for step in STEPS]
+    for i, peer in enumerate(peers):
+        remote(packet, slots.at[i], tile_send.at[0], tile_recv.at[0], peer).start()
+    tell(known.at[2], far)
+
+    vectors = [
+        [xbuf[s]]
+        + [
+            jnp.concatenate(
+                [
+                    jnp.where(upper, edges[s][0][i], inner[s][i][0:8]),
+                    inner[s][i][8:24],
+                    jnp.where(upper, inner[s][i][24:32], edges[s][1][i]),
+                ],
+                axis=0,
+            )
+            for i in range(3)
+        ]
+        for s in range(2)
+    ]
     lane = lax.broadcasted_iota(jnp.int32, (1, LANES), 1)
     low = lane < 64
     surface = []
     for i in range(4):
         both = jnp.where(low, vectors[0][i][:, 0:1], vectors[1][i][:, 0:1])
         surface.append(jnp.sum(jnp.where(here, both, 0.0), axis=0, keepdims=True))
-
-    dots = jnp.sum(jnp.concatenate(rows, axis=0), axis=1, keepdims=True)
-    eye = lax.broadcasted_iota(jnp.int32, (12, LANES), 0) == lax.broadcasted_iota(jnp.int32, (12, LANES), 1)
-    moment_row = jnp.sum(jnp.where(eye, dots, 0.0), axis=0, keepdims=True)
-    packet[...] = jnp.concatenate([moment_row] + surface + [jnp.zeros((3, LANES), jnp.float32)], axis=0)
-    pl.semaphore_wait(known.at[1], len(middle))
-    copies_t = [
-        remote(packet, slots.at[i], tile_send, tile_recv, tile_peer(step)) for i, step in enumerate(STEPS)
-    ]
-    for copy in copies_t:
-        copy.start()
-    tell(known.at[2], far)
-    every = remote(slots, slots, tile_send, tile_recv, (w, below))
+    surfaces[...] = jnp.concatenate(surface, axis=0)
+    for i, peer in enumerate(peers):
+        remote(surfaces, slots_e.at[i], tile_send.at[1], tile_recv.at[1], peer).start()
+
+    every = remote(slots, slots, tile_send.at[0], tile_recv.at[0], (w, below))
+    every_e = remote(slots_e, slots_e, tile_send.at[1], tile_recv.at[1], (w, below))
     every.wait_recv()
     total = packet[...] + jnp.sum(slots[...], axis=0)
     pl.semaphore_wait(known.at[2], len(far))
@@ -299,7 +304,9 @@
     for copy in copies_first:
         copy.start()
 
-    mine[...] = sum(total[1 + i:2 + i] * jnp.where(low, coefs[0][i], coefs[1][i]) for i in range(4))
+    every_e.wait_recv()
+    total_e = surfaces[...] + jnp.sum(slots_e[...], axis=0)
+    mine[...] = sum(total_e[i:i + 1] * jnp.where(low, coefs[0][i], coefs[1][i]) for i in range(4))
     copies_r = [
         remote(mine, slots_r.at[i], r_send, r_recv, wave_peer(i + 1)) for i in range(WAVES - 1)
     ]
@@ -331,7 +338,7 @@
     read[0:1, :] = out_r[:, :64]
     read[1:2, :] = out_r[:, 64:]
 
-    for copy in halos + [every, every_r] + copies_first + copies_second:
+    for copy in halos + [every, every_e, every_r] + copies_first + copies_second:
         copy.wait_send()
 
 
@@ -356,10 +363,12 @@
             pltpu.SMEM((1,), f32),
             pltpu.SMEM((2,), jnp.int32),
             pltpu.SMEM((2,), jnp.int32),
-            pltpu.VMEM((2, 8, COLS + HALF), f32),
-            pltpu.VMEM((2, 8, COLS + HALF), f32),
-            pltpu.VMEM((8, LANES), f32),
-            pltpu.VMEM((TILES - 1, 8, LANES), f32),
+            pltpu.VMEM((2, 8, COLS), jnp.int32),
+            pltpu.VMEM((2, 2, 8, COLS), f32),
+            pltpu.VMEM((1, LANES), f32),
+            pltpu.VMEM((TILES - 1, 1, LANES), f32),
+            pltpu.VMEM((4, LANES), f32),
+            pltpu.VMEM((TILES - 1, 4, LANES), f32),
             pltpu.VMEM((WAVES, ROWS, LANES), f32),
             pltpu.VMEM((n_first, ROWS, LANES), f32),
             pltpu.VMEM((n_second, ROWS, LANES), f32),
@@ -367,15 +376,15 @@
             pltpu.VMEM((1, LANES), f32),
             pltpu.VMEM((WAVES - 1, 1, LANES), f32),
             dma((8,)),
+            dma((4,)), dma((4,)),
             dma((2,)), dma((2,)),
-            dma, dma,
             dma((n_first,)), dma((n_first,)),
             dma((n_second,)), dma((n_second,)),
             dma, dma,
             pltpu.SemaphoreType.REGULAR((3,)),
         ],
         compiler_params=pltpu.CompilerParams(
-            collective_id=0, has_side_effects=True, vmem_limit_bytes=60 * 1024 * 1024
+            collective_id=0, has_side_effects=True, vmem_limit_bytes=55168 * 1024
         ),
     )(warm, cls, cond, wn, wt, srow, scol, erow)
 

time: 40.7 us -> 39.9 us (0.980)
  local copies, waits for them, and re-layouts: 1.94 us -> 1.2 us
    unnamed x4 -> x10, local copies, waits for them, and re-layouts: 1.94 us -> 1.2 us
where the time goes in v3:
time: 39.9 us; the launch traced here: 39.7 us
  Pallas kernels  36.5 us (91%)
  between operations  2.03 us (5%)
  local copies, waits for them, and re-layouts  1.2 us (3%)
    pallas_call x1, Pallas kernels, shards(): pl.pallas_call(kernel, out_shape=(jax.ShapeDtypeStruct((2, ROWS, COLS //...  36.5 us
    unnamed x10, local copies, waits for them, and re-layouts  1.2 us

profile of v3, /device:TPU:32, one launch (start us, length us, event | category | flops | bytes accessed | tf_op | source)
XLA Modules:
  0.0 39.7 jit_solution(9413496638342282430)
XLA Ops:
  0.6 0.0 copy-start.3
  1.3 0.0 copy-start
  1.3 0.0 copy-start.1
  1.3 0.0 copy-start.2
  2.0 0.0 copy-done.3
  2.0 0.0 copy-done
  2.0 0.0 copy-done.1
  2.0 0.0 copy-done.2
  2.0 36.5 %shard_map.95 = (f32[2,32,64]{2,1,0:T(8,128)S(1)}, f32[2,64]{1,0:T(2,128)S(1)}) custom-call(f32[1,2,32,1024]{3,2,1,0:T(8,128)} %warm.1, s32[32,1024]{1,0:T(8,128)} %cls.1, f32[8]{0:T(128)S(1)} %copy-done, f32[1]{0:T(128)S(6)} %copy.12.wn, f32[1]{0:T(128)S(6)} %copy.13.wt, s32[2]{0:T(128)S(1)} %copy-done.1, s32[2]{0:T(128)S(1)} %copy-done.2, s32[64]{0:T(128)S(1)} %copy-done.3), custom_call_target="tpu_custom_call" | custom-call | tf_op jit(solution)/shard_map/pallas_call | solution.py:349
  38.6 0.6 %copy.14 = f32[2,32,64]{2,1,0:T(8,128)} copy(f32[2,32,64]{2,1,0:T(8,128)S(1)} %get-tuple-element.4) | data formatting | bytes 32768
  39.2 0.6 %copy.15 = f32[2,64]{1,0:T(2,128)} copy(f32[2,64]{1,0:T(2,128)S(1)} %get-tuple-element.5) | data formatting | bytes 1024
Async XLA Ops:
  0.6 1.4 %copy-start.3 = (s32[64]{0:T(128)S(1)}, s32[64]{0:T(128)}, u32[]{:S(2)}) copy-start(s32[64]{0:T(128)} %erow.1) | copy-start | bytes 772
  1.3 0.7 %copy-start = (f32[8]{0:T(128)S(1)}, f32[8]{0:T(128)}, u32[]{:S(2)}) copy-start(f32[8]{0:T(128)} %cond.1) | copy-start | bytes 100
  1.3 0.7 %copy-start.1 = (s32[2]{0:T(128)S(1)}, s32[2]{0:T(128)}, u32[]{:S(2)}) copy-start(s32[2]{0:T(128)} %srow.1) | copy-start | bytes 28
  1.3 0.7 %copy-start.2 = (s32[2]{0:T(128)S(1)}, s32[2]{0:T(128)}, u32[]{:S(2)}) copy-start(s32[2]{0:T(128)} %scol.1) | copy-start | bytes 28

commit v4 on v3

--- a/solution.py
+++ b/solution.py
@@ -111,6 +111,8 @@
     for load in loads:
         load.wait()
     sigma = conductivity(cbuf[...])
+    pl.semaphore_wait(known.at[0], len(near))
+    tell(known.at[1], middle)
 
     k = wn_s[0]
 
@@ -134,14 +136,18 @@
         def apply(v, tag):
             return a_up * up(v, tag) + a_down * down(v, tag) + a_left * left(v) + a_right * right(v)
 
-        def chain(x, s):
+        def begin(x, s):
             q = jnp.where((cell_row(row) + t * ROWS == srow_s[s]) & (col == scol_s[s]), SOURCE_STRENGTH, 0.0)
-            v0 = q * inv - x + apply(x, (s, 0))
-            v1 = apply(v0, (s, 1))
-            v2 = apply(v1, (s, 2))
-            return v0, v1, v2, apply(v2, (s, 3))
-
-        return diag, chain
+            return q * inv - x + apply(x, (s, 0))
+
+        return diag, begin, apply
+
+    def chains(work):
+        v0 = [st[1](x, s) for st, x, s in work]
+        v1 = [st[2](v, (s, 1)) for (st, _, s), v in zip(work, v0)]
+        v2 = [st[2](v, (s, 2)) for (st, _, s), v in zip(work, v1)]
+        v3 = [st[2](v, (s, 3)) for (st, _, s), v in zip(work, v2)]
+        return list(zip(v0, v1, v2, v3))
 
     def fold(product):
         total = product[:, :LANES]
@@ -157,16 +163,16 @@
     upper = sub < 4
     upper_lanes = lax.broadcasted_iota(jnp.int32, (8, LANES), 0) < 4
 
-    diag, chain = stencil(
+    whole = stencil(
         sigma,
         lambda row: row,
         lambda v, tag: pltpu.roll(v, 1, 0),
         lambda v, tag: pltpu.roll(v, ROWS - 1, 0),
         None,
     )
-    inner = [chain(xbuf[s], s) for s in range(2)]
+    inner = chains([(whole, xbuf[s], s) for s in range(2)])
     inner_moments = [
-        [f[8:16] + f[16:24] + jnp.where(upper_lanes, f[24:32], f[0:8]) for f in moments(diag, *inner[s])]
+        [f[8:16] + f[16:24] + jnp.where(upper_lanes, f[24:32], f[0:8]) for f in moments(whole[0], *inner[s])]
         for s in range(2)
     ]
     own = {0: (sigma[0:8], sigma[24:32])}
@@ -181,8 +187,8 @@
 
     for copy in halos:
         copy.wait_recv()
-    pl.semaphore_wait(known.at[0], len(near))
-    tell(known.at[1], middle)
+    pl.semaphore_wait(known.at[1], len(middle))
+    tell(known.at[2], far)
 
     edge_stencil = [
         stencil(
@@ -200,26 +206,25 @@
             (jnp.where(t == TILES - 1, 0, -1), jnp.where(t == TILES - 1, 7, -1)),
         ),
     ]
-    edges = []
+    outer = chains(
+        [(edge_stencil[0], jnp.where(upper, own[(s, 0)][0], halo_x[1, s]), s) for s in range(2)]
+        + [(edge_stencil[1], jnp.where(upper, halo_x[0, s], own[(s, 0)][1]), s) for s in range(2)]
+    )
+    edges = [(outer[s], outer[2 + s]) for s in range(2)]
     rows = []
     for s in range(2):
-        block0 = edge_stencil[0][1](jnp.where(upper, own[(s, 0)][0], halo_x[1, s]), s)
-        block1 = edge_stencil[1][1](jnp.where(upper, halo_x[0, s], own[(s, 0)][1]), s)
-        outer = zip(moments(edge_stencil[0][0], *block0), moments(edge_stencil[1][0], *block1))
+        pairs = zip(moments(edge_stencil[0][0], *edges[s][0]), moments(edge_stencil[1][0], *edges[s][1]))
         rows += [
             jnp.sum(a + jnp.where(upper_lanes, b, c), axis=0, keepdims=True)
-            for a, (b, c) in zip(inner_moments[s], outer)
+            for a, (b, c) in zip(inner_moments[s], pairs)
         ]
-        edges.append((block0, block1))
 
     dots = jnp.sum(jnp.concatenate(rows, axis=0), axis=1, keepdims=True)
     eye = lax.broadcasted_iota(jnp.int32, (12, LANES), 0) == lax.broadcasted_iota(jnp.int32, (12, LANES), 1)
     packet[...] = jnp.sum(jnp.where(eye, dots, 0.0), axis=0, keepdims=True)
-    pl.semaphore_wait(known.at[1], len(middle))
     peers = [tile_peer(step) for step in STEPS]
     for i, peer in enumerate(peers):
         remote(packet, slots.at[i], tile_send.at[0], tile_recv.at[0], peer).start()
-    tell(known.at[2], far)
 
     vectors = [
         [xbuf[s]]

time: 39.9 us -> 38.4 us (0.962)
  Pallas kernels: 36.5 us -> 35 us
    pallas_call x1, Pallas kernels: 36.5 us -> 35 us  [shards(): pl.pallas_call(kernel, out_shape=(jax.ShapeDtypeStruct((2, ROWS, COLS //...]
where the time goes in v4:
time: 38.4 us; the launch traced here: 38.2 us
  Pallas kernels  35 us (91%)
  between operations  2.03 us (5%)
  local copies, waits for them, and re-layouts  1.2 us (3%)
    pallas_call x1, Pallas kernels, shards(): pl.pallas_call(kernel, out_shape=(jax.ShapeDtypeStruct((2, ROWS, COLS //...  35 us
    unnamed x10, local copies, waits for them, and re-layouts  1.2 us

profile of v4, /device:TPU:32, one launch (start us, length us, event | category | flops | bytes accessed | tf_op | source)
XLA Modules:
  0.0 38.2 jit_solution(3797579334278147121)
XLA Ops:
  0.6 0.0 copy-start.3
  1.3 0.0 copy-start
  1.3 0.0 copy-start.1
  1.3 0.0 copy-start.2
  2.0 0.0 copy-done.3
  2.0 0.0 copy-done
  2.0 0.0 copy-done.1
  2.0 0.0 copy-done.2
  2.0 35.0 %shard_map.95 = (f32[2,32,64]{2,1,0:T(8,128)S(1)}, f32[2,64]{1,0:T(2,128)S(1)}) custom-call(f32[1,2,32,1024]{3,2,1,0:T(8,128)} %warm.1, s32[32,1024]{1,0:T(8,128)} %cls.1, f32[8]{0:T(128)S(1)} %copy-done, f32[1]{0:T(128)S(6)} %copy.12.wn, f32[1]{0:T(128)S(6)} %copy.13.wt, s32[2]{0:T(128)S(1)} %copy-done.1, s32[2]{0:T(128)S(1)} %copy-done.2, s32[64]{0:T(128)S(1)} %copy-done.3), custom_call_target="tpu_custom_call" | custom-call | tf_op jit(solution)/shard_map/pallas_call | solution.py:354
  37.1 0.6 %copy.14 = f32[2,32,64]{2,1,0:T(8,128)} copy(f32[2,32,64]{2,1,0:T(8,128)S(1)} %get-tuple-element.4) | data formatting | bytes 32768
  37.7 0.6 %copy.15 = f32[2,64]{1,0:T(2,128)} copy(f32[2,64]{1,0:T(2,128)S(1)} %get-tuple-element.5) | data formatting | bytes 1024
Async XLA Ops:
  0.6 1.4 %copy-start.3 = (s32[64]{0:T(128)S(1)}, s32[64]{0:T(128)}, u32[]{:S(2)}) copy-start(s32[64]{0:T(128)} %erow.1) | copy-start | bytes 772
  1.3 0.7 %copy-start = (f32[8]{0:T(128)S(1)}, f32[8]{0:T(128)}, u32[]{:S(2)}) copy-start(f32[8]{0:T(128)} %cond.1) | copy-start | bytes 100
  1.3 0.7 %copy-start.1 = (s32[2]{0:T(128)S(1)}, s32[2]{0:T(128)}, u32[]{:S(2)}) copy-start(s32[2]{0:T(128)} %srow.1) | copy-start | bytes 28
  1.3 0.7 %copy-start.2 = (s32[2]{0:T(128)S(1)}, s32[2]{0:T(128)}, u32[]{:S(2)}) copy-start(s32[2]{0:T(128)} %scol.1) | copy-start | bytes 28

commit v5 on v4

--- a/solution.py
+++ b/solution.py
@@ -6,6 +6,7 @@
 from jax.sharding import PartitionSpec as P
 
 SOURCE_STRENGTH = 50.0
+N_FAR_R = 7
 MESH = pl.DeviceIdType.MESH
 
 WAVES = 16
@@ -14,9 +15,9 @@
 COLS = 1024
 LANES = 128
 
-FIRST = {7: (6, 8), -7: (-6,), 4: (3, 5), -4: (-3, -5), 2: (1,), -2: (-1,)}
+FIRST = {6: (8, 7, 5), -6: (-7, -5), 3: (4, 2), -3: (-4, -2), 0: (1, -1)}
 FIRST_LIST = [(c, o) for c, offsets in FIRST.items() for o in offsets]
-SECOND_LIST = list(FIRST)
+SECOND_LIST = [c for c in FIRST if c != 0]
 
 STEPS = sorted(
     [(a, b, c) for a in range(4) for b in range(4) for c in range(2) if (a, b, c) != (0, 0, 0)],
@@ -219,13 +220,6 @@
             for a, (b, c) in zip(inner_moments[s], pairs)
         ]
 
-    dots = jnp.sum(jnp.concatenate(rows, axis=0), axis=1, keepdims=True)
-    eye = lax.broadcasted_iota(jnp.int32, (12, LANES), 0) == lax.broadcasted_iota(jnp.int32, (12, LANES), 1)
-    packet[...] = jnp.sum(jnp.where(eye, dots, 0.0), axis=0, keepdims=True)
-    peers = [tile_peer(step) for step in STEPS]
-    for i, peer in enumerate(peers):
-        remote(packet, slots.at[i], tile_send.at[0], tile_recv.at[0], peer).start()
-
     vectors = [
         [xbuf[s]]
         + [
@@ -248,6 +242,13 @@
         both = jnp.where(low, vectors[0][i][:, 0:1], vectors[1][i][:, 0:1])
         surface.append(jnp.sum(jnp.where(here, both, 0.0), axis=0, keepdims=True))
     surfaces[...] = jnp.concatenate(surface, axis=0)
+
+    dots = jnp.sum(jnp.concatenate(rows, axis=0), axis=1, keepdims=True)
+    eye = lax.broadcasted_iota(jnp.int32, (12, LANES), 0) == lax.broadcasted_iota(jnp.int32, (12, LANES), 1)
+    packet[...] = jnp.sum(jnp.where(eye, dots, 0.0), axis=0, keepdims=True)
+    peers = [tile_peer(step) for step in STEPS]
+    for i, peer in enumerate(peers):
+        remote(packet, slots.at[i], tile_send.at[0], tile_recv.at[0], peer).start()
     for i, peer in enumerate(peers):
         remote(surfaces, slots_e.at[i], tile_send.at[1], tile_recv.at[1], peer).start()
 
@@ -306,17 +307,18 @@
         )
         for i, (c, o) in enumerate(FIRST_LIST)
     ]
-    for copy in copies_first:
-        copy.start()
-
     every_e.wait_recv()
     total_e = surfaces[...] + jnp.sum(slots_e[...], axis=0)
     mine[...] = sum(total_e[i:i + 1] * jnp.where(low, coefs[0][i], coefs[1][i]) for i in range(4))
-    copies_r = [
-        remote(mine, slots_r.at[i], r_send, r_recv, wave_peer(i + 1)) for i in range(WAVES - 1)
-    ]
-    for copy in copies_r:
+    copies_r = [remote(mine, slots_r.at[i], r_send, r_recv, wave_peer(i + 1)) for i in range(WAVES - 1)]
+    order = sorted(range(WAVES - 1), key=lambda i: -min(i + 1, WAVES - 1 - i))
+    for i in order[:N_FAR_R]:
+        copies_r[i].start()
+    for copy in copies_first:
         copy.start()
+
+    for i in order[N_FAR_R:]:
+        copies_r[i].start()
 
     copies_second = []
     for j, c in enumerate(SECOND_LIST):
@@ -332,33 +334,42 @@
     every_r = remote(slots_r, slots_r, r_send, r_recv, wave_peer(1))
 
     acc = chunks[w]
+    for i, (c, o) in enumerate(FIRST_LIST):
+        if c == 0:
+            copies_first[i].wait_recv()
+            acc = acc + got_first[i]
     for j in reversed(range(len(SECOND_LIST))):
         copies_second[j].wait_recv()
         acc = acc + got_second[j]
-    pot[0] = acc[:, :64]
-    pot[1] = acc[:, 64:]
+    pot[...] = acc
 
     every_r.wait_recv()
-    out_r = mine[...] + jnp.sum(slots_r[...], axis=0)
-    read[0:1, :] = out_r[:, :64]
-    read[1:2, :] = out_r[:, 64:]
+    read[...] = mine[...] + jnp.sum(slots_r[...], axis=0)
 
     for copy in halos + [every, every_e, every_r] + copies_first + copies_second:
         copy.wait_send()
 
 
+def part(both, both_r, pot, read):
+    pot[0] = both[:, :64]
+    pot[1] = both[:, 64:]
+    read[0:1, :] = both_r[:, :64]
+    read[1:2, :] = both_r[:, 64:]
+
+
 def shards(warm, cls, cond, wn, wt, srow, scol, erow):
     f32 = jnp.float32
+    in_vmem = pl.BlockSpec(memory_space=pltpu.VMEM)
     dma = pltpu.SemaphoreType.DMA
     n_first, n_second = len(FIRST_LIST), len(SECOND_LIST)
-    return pl.pallas_call(
+    both = pl.pallas_call(
         kernel,
         out_shape=(
-            jax.ShapeDtypeStruct((2, ROWS, COLS // WAVES), f32),
-            jax.ShapeDtypeStruct((2, 64), f32),
+            jax.ShapeDtypeStruct((ROWS, LANES), f32),
+            jax.ShapeDtypeStruct((1, LANES), f32),
         ),
         in_specs=[pl.BlockSpec(memory_space=pltpu.HBM)] * 8,
-        out_specs=[pl.BlockSpec(memory_space=pltpu.VMEM)] * 2,
+        out_specs=[in_vmem] * 2,
         scratch_shapes=[
             pltpu.VMEM((2, ROWS, COLS), f32),
             pltpu.VMEM((ROWS, COLS), jnp.int32),
@@ -392,6 +403,16 @@
             collective_id=0, has_side_effects=True, vmem_limit_bytes=55168 * 1024
         ),
     )(warm, cls, cond, wn, wt, srow, scol, erow)
+    return pl.pallas_call(
+        part,
+        out_shape=(
+            jax.ShapeDtypeStruct((2, ROWS, COLS // WAVES), f32),
+            jax.ShapeDtypeStruct((2, 64), f32),
+        ),
+        in_specs=[in_vmem] * 2,
+        out_specs=[in_vmem] * 2,
+        compiler_params=pltpu.CompilerParams(vmem_limit_bytes=55168 * 1024),
+    )(*both)
 
 
 def solution(mesh):

time: 38.4 us -> 36.7 us (0.956)
  local copies, waits for them, and re-layouts: 1.2 us -> 0.02 us
  Pallas kernels: 35 us -> 34.5 us
    unnamed x10 -> x8, local copies, waits for them, and re-layouts: 1.2 us -> 0.02 us
    pallas_call x1 -> x2, Pallas kernels: 35 us -> 34.5 us  [the longest x1 33.9 us: shards(): pl.pallas_call(kernel, out_shape=(jax.ShapeDtypeStruct((ROWS, LANES), f32...]
where the time goes in v5:
time: 36.7 us; the launch traced here: 36.6 us
  Pallas kernels  34.5 us (94%)
  between operations  2.03 us (6%)
    pallas_call x1, Pallas kernels, shards(): pl.pallas_call(kernel, out_shape=(jax.ShapeDtypeStruct((ROWS, LANES), f32...  33.9 us

profile of v5, /device:TPU:32, one launch (start us, length us, event | category | flops | bytes accessed | tf_op | source)
XLA Modules:
  0.0 36.6 jit_solution(7831888913860288642)
XLA Ops:
  0.6 0.0 copy-start.3
  1.3 0.0 copy-start
  1.3 0.0 copy-start.1
  1.3 0.0 copy-start.2
  2.0 0.0 copy-done.3
  2.0 0.0 copy-done
  2.0 0.0 copy-done.1
  2.0 0.0 copy-done.2
  2.0 33.9 %shard_map.95 = (f32[32,128]{1,0:T(8,128)S(1)}, f32[1,128]{1,0:T(1,128)S(1)}) custom-call(f32[1,2,32,1024]{3,2,1,0:T(8,128)} %warm.1, s32[32,1024]{1,0:T(8,128)} %cls.1, f32[8]{0:T(128)S(1)} %copy-done, f32[1]{0:T(128)S(6)} %copy.10.wn, f32[1]{0:T(128)S(6)} %copy.11.wt, s32[2]{0:T(128)S(1)} %copy-done.1, s32[2]{0:T(128)S(1)} %copy-done.2, s32[64]{0:T(128)S(1)} %copy-done.3), custom_call_target="tpu_custom_call" | custom-call | tf_op jit(solution)/shard_map/pallas_call | solution.py:365
  35.9 0.7 %shard_map.96 = (f32[2,32,64]{2,1,0:T(8,128)}, f32[2,64]{1,0:T(2,128)}) custom-call(f32[32,128]{1,0:T(8,128)S(1)} %get-tuple-element.4.both, f32[1,128]{1,0:T(1,128)S(1)} %get-tuple-element.5.both_r), custom_call_target="tpu_custom_call" | custom-call | tf_op jit(solution)/shard_map/pallas_call | solution.py:406
Async XLA Ops:
  0.6 1.4 %copy-start.3 = (s32[64]{0:T(128)S(1)}, s32[64]{0:T(128)}, u32[]{:S(2)}) copy-start(s32[64]{0:T(128)} %erow.1) | copy-start | bytes 772
  1.3 0.7 %copy-start = (f32[8]{0:T(128)S(1)}, f32[8]{0:T(128)}, u32[]{:S(2)}) copy-start(f32[8]{0:T(128)} %cond.1) | copy-start | bytes 100
  1.3 0.7 %copy-start.1 = (s32[2]{0:T(128)S(1)}, s32[2]{0:T(128)}, u32[]{:S(2)}) copy-start(s32[2]{0:T(128)} %srow.1) | copy-start | bytes 28
  1.3 0.7 %copy-start.2 = (s32[2]{0:T(128)S(1)}, s32[2]{0:T(128)}, u32[]{:S(2)}) copy-start(s32[2]{0:T(128)} %scol.1) | copy-start | bytes 28

commit v6 on v5

--- a/solution.py
+++ b/solution.py
@@ -307,6 +307,8 @@
         )
         for i, (c, o) in enumerate(FIRST_LIST)
     ]
+    for copy in copies_first:
+        copy.start()
     every_e.wait_recv()
     total_e = surfaces[...] + jnp.sum(slots_e[...], axis=0)
     mine[...] = sum(total_e[i:i + 1] * jnp.where(low, coefs[0][i], coefs[1][i]) for i in range(4))
@@ -314,8 +316,6 @@
     order = sorted(range(WAVES - 1), key=lambda i: -min(i + 1, WAVES - 1 - i))
     for i in order[:N_FAR_R]:
         copies_r[i].start()
-    for copy in copies_first:
-        copy.start()
 
     for i in order[N_FAR_R:]:
         copies_r[i].start()

time: 36.7 us -> 36.5 us (level)
  the two profiles are of different devices: /device:TPU:32 before, /device:TPU:1 now
where the time goes in v6:
time: 36.5 us; the launch traced here: 36.3 us
  Pallas kernels  34.3 us (94%)
  between operations  2.03 us (6%)
    pallas_call x1, Pallas kernels, shards(): pl.pallas_call(kernel, out_shape=(jax.ShapeDtypeStruct((ROWS, LANES), f32...  33.6 us

profile of v6, /device:TPU:1, one launch (start us, length us, event | category | flops | bytes accessed | tf_op | source)
XLA Modules:
  0.0 36.3 jit_solution(7331587580525131304)
XLA Ops:
  0.6 0.0 copy-start.3
  1.3 0.0 copy-start
  1.3 0.0 copy-start.1
  1.3 0.0 copy-start.2
  2.0 0.0 copy-done.3
  2.0 0.0 copy-done
  2.0 0.0 copy-done.1
  2.0 0.0 copy-done.2
  2.0 33.6 %shard_map.95 = (f32[32,128]{1,0:T(8,128)S(1)}, f32[1,128]{1,0:T(1,128)S(1)}) custom-call(f32[1,2,32,1024]{3,2,1,0:T(8,128)} %warm.1, s32[32,1024]{1,0:T(8,128)} %cls.1, f32[8]{0:T(128)S(1)} %copy-done, f32[1]{0:T(128)S(6)} %copy.10.wn, f32[1]{0:T(128)S(6)} %copy.11.wt, s32[2]{0:T(128)S(1)} %copy-done.1, s32[2]{0:T(128)S(1)} %copy-done.2, s32[64]{0:T(128)S(1)} %copy-done.3), custom_call_target="tpu_custom_call" | custom-call | tf_op jit(solution)/shard_map/pallas_call | solution.py:365
  35.6 0.7 %shard_map.96 = (f32[2,32,64]{2,1,0:T(8,128)}, f32[2,64]{1,0:T(2,128)}) custom-call(f32[32,128]{1,0:T(8,128)S(1)} %get-tuple-element.4.both, f32[1,128]{1,0:T(1,128)S(1)} %get-tuple-element.5.both_r), custom_call_target="tpu_custom_call" | custom-call | tf_op jit(solution)/shard_map/pallas_call | solution.py:406
Async XLA Ops:
  0.6 1.4 %copy-start.3 = (s32[64]{0:T(128)S(1)}, s32[64]{0:T(128)}, u32[]{:S(2)}) copy-start(s32[64]{0:T(128)} %erow.1) | copy-start | bytes 772
  1.3 0.7 %copy-start = (f32[8]{0:T(128)S(1)}, f32[8]{0:T(128)}, u32[]{:S(2)}) copy-start(f32[8]{0:T(128)} %cond.1) | copy-start | bytes 100
  1.3 0.7 %copy-start.1 = (s32[2]{0:T(128)S(1)}, s32[2]{0:T(128)}, u32[]{:S(2)}) copy-start(s32[2]{0:T(128)} %srow.1) | copy-start | bytes 28
  1.3 0.7 %copy-start.2 = (s32[2]{0:T(128)S(1)}, s32[2]{0:T(128)}, u32[]{:S(2)}) copy-start(s32[2]{0:T(128)} %scol.1) | copy-start | bytes 28

commit v7 on v6

--- a/solution.py
+++ b/solution.py
@@ -220,6 +220,12 @@
             for a, (b, c) in zip(inner_moments[s], pairs)
         ]
 
+    dots = jnp.sum(jnp.concatenate(rows, axis=0), axis=1, keepdims=True)
+    eye = lax.broadcasted_iota(jnp.int32, (12, LANES), 0) == lax.broadcasted_iota(jnp.int32, (12, LANES), 1)
+    packet[...] = jnp.sum(jnp.where(eye, dots, 0.0), axis=0, keepdims=True)
+    peers = [tile_peer(step) for step in STEPS]
+    for i, peer in enumerate(peers):
+        remote(packet, slots.at[i], tile_send.at[0], tile_recv.at[0], peer).start()
     vectors = [
         [xbuf[s]]
         + [
@@ -242,13 +248,6 @@
         both = jnp.where(low, vectors[0][i][:, 0:1], vectors[1][i][:, 0:1])
         surface.append(jnp.sum(jnp.where(here, both, 0.0), axis=0, keepdims=True))
     surfaces[...] = jnp.concatenate(surface, axis=0)
-
-    dots = jnp.sum(jnp.concatenate(rows, axis=0), axis=1, keepdims=True)
-    eye = lax.broadcasted_iota(jnp.int32, (12, LANES), 0) == lax.broadcasted_iota(jnp.int32, (12, LANES), 1)
-    packet[...] = jnp.sum(jnp.where(eye, dots, 0.0), axis=0, keepdims=True)
-    peers = [tile_peer(step) for step in STEPS]
-    for i, peer in enumerate(peers):
-        remote(packet, slots.at[i], tile_send.at[0], tile_recv.at[0], peer).start()
     for i, peer in enumerate(peers):
         remote(surfaces, slots_e.at[i], tile_send.at[1], tile_recv.at[1], peer).start()
 

time: 36.5 us -> 36.6 us (level)
  no operation moved by 1% of the time
where the time goes in v7:
time: 36.6 us; the launch traced here: 36.5 us
  Pallas kernels  34.4 us (94%)
  between operations  2.03 us (6%)
    pallas_call x1, Pallas kernels, shards(): pl.pallas_call(kernel, out_shape=(jax.ShapeDtypeStruct((ROWS, LANES), f32...  33.7 us

profile of v7, /device:TPU:1, one launch (start us, length us, event | category | flops | bytes accessed | tf_op | source)
XLA Modules:
  0.0 36.5 jit_solution(4632066840612891103)
XLA Ops:
  0.6 0.0 copy-start.3
  1.3 0.0 copy-start
  1.3 0.0 copy-start.1
  1.3 0.0 copy-start.2
  2.0 0.0 copy-done.3
  2.0 0.0 copy-done
  2.0 0.0 copy-done.1
  2.0 0.0 copy-done.2
  2.0 33.7 %shard_map.95 = (f32[32,128]{1,0:T(8,128)S(1)}, f32[1,128]{1,0:T(1,128)S(1)}) custom-call(f32[1,2,32,1024]{3,2,1,0:T(8,128)} %warm.1, s32[32,1024]{1,0:T(8,128)} %cls.1, f32[8]{0:T(128)S(1)} %copy-done, f32[1]{0:T(128)S(6)} %copy.10.wn, f32[1]{0:T(128)S(6)} %copy.11.wt, s32[2]{0:T(128)S(1)} %copy-done.1, s32[2]{0:T(128)S(1)} %copy-done.2, s32[64]{0:T(128)S(1)} %copy-done.3), custom_call_target="tpu_custom_call" | custom-call | tf_op jit(solution)/shard_map/pallas_call | solution.py:364
  35.8 0.7 %shard_map.96 = (f32[2,32,64]{2,1,0:T(8,128)}, f32[2,64]{1,0:T(2,128)}) custom-call(f32[32,128]{1,0:T(8,128)S(1)} %get-tuple-element.4.both, f32[1,128]{1,0:T(1,128)S(1)} %get-tuple-element.5.both_r), custom_call_target="tpu_custom_call" | custom-call | tf_op jit(solution)/shard_map/pallas_call | solution.py:405
Async XLA Ops:
  0.6 1.4 %copy-start.3 = (s32[64]{0:T(128)S(1)}, s32[64]{0:T(128)}, u32[]{:S(2)}) copy-start(s32[64]{0:T(128)} %erow.1) | copy-start | bytes 772
  1.3 0.7 %copy-start = (f32[8]{0:T(128)S(1)}, f32[8]{0:T(128)}, u32[]{:S(2)}) copy-start(f32[8]{0:T(128)} %cond.1) | copy-start | bytes 100
  1.3 0.7 %copy-start.1 = (s32[2]{0:T(128)S(1)}, s32[2]{0:T(128)}, u32[]{:S(2)}) copy-start(s32[2]{0:T(128)} %srow.1) | copy-start | bytes 28
  1.3 0.7 %copy-start.2 = (s32[2]{0:T(128)S(1)}, s32[2]{0:T(128)}, u32[]{:S(2)}) copy-start(s32[2]{0:T(128)} %scol.1) | copy-start | bytes 28

commit v8 on v7

--- a/solution.py
+++ b/solution.py
@@ -91,12 +91,12 @@
             src_ref=src, dst_ref=dst, send_sem=send, recv_sem=recv, device_id=device, device_id_type=MESH
         )
 
-    first, final = pl.ds(0, 8), pl.ds(ROWS - 8, 8)
+    first, final, lower = pl.ds(0, 4), pl.ds(ROWS - 4, 4), pl.ds(4, 4)
     halos = [
-        remote(cls.at[first], halo_c.at[0], halo_send.at[0], halo_recv.at[0], (w, above)),
-        remote(cls.at[final], halo_c.at[1], halo_send.at[1], halo_recv.at[1], (w, below)),
-        remote(warm.at[0, :, first], halo_x.at[0], halo_send.at[2], halo_recv.at[2], (w, above)),
-        remote(warm.at[0, :, final], halo_x.at[1], halo_send.at[3], halo_recv.at[3], (w, below)),
+        remote(cls.at[first], halo_c.at[0, first], halo_send.at[0], halo_recv.at[0], (w, above)),
+        remote(cls.at[final], halo_c.at[1, lower], halo_send.at[1], halo_recv.at[1], (w, below)),
+        remote(warm.at[0, :, first], halo_x.at[0, :, first], halo_send.at[2], halo_recv.at[2], (w, above)),
+        remote(warm.at[0, :, final], halo_x.at[1, :, lower], halo_send.at[3], halo_recv.at[3], (w, below)),
     ]
     pl.semaphore_wait(barrier, len(near))
     for copy in halos:

time: 36.6 us -> 37 us (1.011)
  the two profiles are of different devices: /device:TPU:1 before, /device:TPU:8 now
where the time goes in v8:
time: 37 us; the launch traced here: 36.8 us
  Pallas kernels  34.8 us (94%)
  between operations  2.03 us (5%)
    pallas_call x1, Pallas kernels, shards(): pl.pallas_call(kernel, out_shape=(jax.ShapeDtypeStruct((ROWS, LANES), f32...  34.1 us

profile of v8, /device:TPU:8, one launch (start us, length us, event | category | flops | bytes accessed | tf_op | source)
XLA Modules:
  0.0 36.8 jit_solution(8726751682657835682)
XLA Ops:
  0.6 0.0 copy-start.3
  1.3 0.0 copy-start
  1.3 0.0 copy-start.1
  1.3 0.0 copy-start.2
  2.0 0.0 copy-done.3
  2.0 0.0 copy-done
  2.0 0.0 copy-done.1
  2.0 0.0 copy-done.2
  2.0 34.1 %shard_map.95 = (f32[32,128]{1,0:T(8,128)S(1)}, f32[1,128]{1,0:T(1,128)S(1)}) custom-call(f32[1,2,32,1024]{3,2,1,0:T(8,128)} %warm.1, s32[32,1024]{1,0:T(8,128)} %cls.1, f32[8]{0:T(128)S(1)} %copy-done, f32[1]{0:T(128)S(6)} %copy.10.wn, f32[1]{0:T(128)S(6)} %copy.11.wt, s32[2]{0:T(128)S(1)} %copy-done.1, s32[2]{0:T(128)S(1)} %copy-done.2, s32[64]{0:T(128)S(1)} %copy-done.3), custom_call_target="tpu_custom_call" | custom-call | tf_op jit(solution)/shard_map/pallas_call | solution.py:364
  36.1 0.7 %shard_map.96 = (f32[2,32,64]{2,1,0:T(8,128)}, f32[2,64]{1,0:T(2,128)}) custom-call(f32[32,128]{1,0:T(8,128)S(1)} %get-tuple-element.4.both, f32[1,128]{1,0:T(1,128)S(1)} %get-tuple-element.5.both_r), custom_call_target="tpu_custom_call" | custom-call | tf_op jit(solution)/shard_map/pallas_call | solution.py:405
Async XLA Ops:
  0.6 1.4 %copy-start.3 = (s32[64]{0:T(128)S(1)}, s32[64]{0:T(128)}, u32[]{:S(2)}) copy-start(s32[64]{0:T(128)} %erow.1) | copy-start | bytes 772
  1.3 0.7 %copy-start = (f32[8]{0:T(128)S(1)}, f32[8]{0:T(128)}, u32[]{:S(2)}) copy-start(f32[8]{0:T(128)} %cond.1) | copy-start | bytes 100
  1.3 0.7 %copy-start.1 = (s32[2]{0:T(128)S(1)}, s32[2]{0:T(128)}, u32[]{:S(2)}) copy-start(s32[2]{0:T(128)} %srow.1) | copy-start | bytes 28
  1.3 0.7 %copy-start.2 = (s32[2]{0:T(128)S(1)}, s32[2]{0:T(128)}, u32[]{:S(2)}) copy-start(s32[2]{0:T(128)} %scol.1) | copy-start | bytes 28
